TPU v7x, 32 devices: a whole 2x2x4 slice. The times are simulated.
32 devices in a mesh: dp: 16 (over z, x, core), mp: 2 (over y).
Axes of the slice: x: 2, y: 2, z: 4, core: 2. Of those that a mesh axis runs over, the one named last changes fastest.
Arguments:
- tokens: bfloat16 [2, 1024, 1024], P(None, 'dp'), may hold values from -6 to 6
- cotangent: bfloat16 [2, 1024, 1024], P(None, 'dp'), may hold values from -6 to 6
- segments: int32 [2, 1024], P(None, 'dp'), may hold values from 0 to 63, as said below
- w_qkv: float32 [3, 1024, 1024], P(None, 'dp', 'mp'), may hold values from -0.1875 to 0.1875
- w_out: float32 [1024, 1024], P('mp', 'dp'), may hold values from -0.75 to 0.75
- w_fc: float32 [1024, 4096], P('dp', 'mp'), may hold values from -0.1875 to 0.1875
- w_proj: float32 [4096, 1024], P('mp', 'dp'), may hold values from -0.09375 to 0.09375
- vec_norm: float32 [6, 1024], P(None, 'dp'), may hold values from -0.8 to 1.4, as said below
- vec_split: float32 [6, 1024], P(None, ('mp', 'dp')), may hold values from -1.2 to 1.2
- first_qkv: float32 [3, 1024, 1024], P(None, 'dp', 'mp'), may hold values from -32 to 32
- first_out: float32 [1024, 1024], P('mp', 'dp'), may hold values from -6 to 6
- first_fc: float32 [1024, 4096], P('dp', 'mp'), may hold values from -8 to 8
- first_proj: float32 [4096, 1024], P('mp', 'dp'), may hold values from -20 to 20
- first_norm: float32 [6, 1024], P(None, 'dp'), may hold values from -32 to 32
- first_split: float32 [6, 1024], P(None, ('mp', 'dp')), may hold values from -16 to 16
- second_qkv: float32 [3, 1024, 1024], P(None, 'dp', 'mp'), may hold values from 108.544 to 430.08
- second_out: float32 [1024, 1024], P('mp', 'dp'), may hold values from 4.3008 to 17.2032
- second_fc: float32 [1024, 4096], P('dp', 'mp'), may hold values from 9.8304 to 38.912
- second_proj: float32 [4096, 1024], P('mp', 'dp'), may hold values from 45.056 to 182.272
- second_norm: float32 [6, 1024], P(None, 'dp'), may hold values from 108.544 to 430.08
- second_split: float32 [6, 1024], P(None, ('mp', 'dp')), may hold values from 38.912 to 155.648
Outputs:
- out_tokens: bfloat16 [2, 1024, 1024], P(None, 'dp')
- in_grad: bfloat16 [2, 1024, 1024], P(None, 'dp')
- next_qkv: float32 [3, 1024, 1024], P(None, 'dp', 'mp')
- next_out: float32 [1024, 1024], P('mp', 'dp')
- next_fc: float32 [1024, 4096], P('dp', 'mp')
- next_proj: float32 [4096, 1024], P('mp', 'dp')
- next_norm: float32 [6, 1024], P(None, 'dp')
- next_split: float32 [6, 1024], P(None, ('mp', 'dp'))
- moment_qkv: float32 [3, 1024, 1024], P(None, 'dp', 'mp')
- moment_out: float32 [1024, 1024], P('mp', 'dp')
- moment_fc: float32 [1024, 4096], P('dp', 'mp')
- moment_proj: float32 [4096, 1024], P('mp', 'dp')
- moment_norm: float32 [6, 1024], P(None, 'dp')
- moment_split: float32 [6, 1024], P(None, ('mp', 'dp'))
- square_qkv: float32 [3, 1024, 1024], P(None, 'dp', 'mp')
- square_out: float32 [1024, 1024], P('mp', 'dp')
- square_fc: float32 [1024, 4096], P('dp', 'mp')
- square_proj: float32 [4096, 1024], P('mp', 'dp')
- square_norm: float32 [6, 1024], P(None, 'dp')
- square_split: float32 [6, 1024], P(None, ('mp', 'dp'))
Inputs may be any that keep to these rules, and one draw needn't show every extreme that they name: `segments`: within each block of 64 positions (one micro-batch, one index of dp) the numbers start at 0, never fall and rise by at most one from a position to the next; equal numbers in a block form one sequence. In every draw some block holds a single sequence, and another block holds 64 sequences of one token. `vec_norm`: rows 0 and 2 are norm gains near one; the other rows are biases.
All inputs are finite; a program needn't handle non-finite values.
Results may differ from a plain program's by a relative error of at most 0.015.
Values may be sent and summed in bfloat16 or wider, within the bound.
A program may use at most 128 MiB of HBM per device.

v0:
```python
import math

import jax
import jax.numpy as jnp
from jax import lax
from jax.sharding import PartitionSpec as P

D = 1024
HD = 64
FF = 4096
TOK_MB = 64
STEP = 10


def layer_norm(values, gain_row, shift_row):
    center = values - jnp.mean(values, axis=-1, keepdims=True)
    spread = jnp.mean(center * center, axis=-1, keepdims=True)
    return center * lax.rsqrt(spread + 1e-05) * gain_row + shift_row


def smooth_gate(values):
    return jax.nn.gelu(values, approximate=True)


def rate_list():
    narrow = D // min(32, max(2, TOK_MB // 4))
    return (
        2.0 / math.sqrt(D),
        2.0 / math.sqrt(narrow),
        2.0 / math.sqrt(D),
        2.0 / math.sqrt(FF),
        0.8,
        0.4,
    )


def adamw(weight, gradient, first_moment, second, step_rate, weight_decay):
    first_new = 0.9 * first_moment + 0.1 * gradient
    second_new = 0.95 * second + 0.05 * gradient * gradient
    scaled_first = first_new / (1.0 - 0.9**STEP)
    scaled_second = second_new / (1.0 - 0.95**STEP)
    weight_new = weight - step_rate * (
        scaled_first / (jnp.sqrt(scaled_second) + 1e-08) + weight_decay * weight
    )
    return (weight_new, first_new, second_new)


def masked_scores(query_heads, key_heads, allowed):
    scores = (
        jnp.einsum("qhd,khd->hqk", query_heads, key_heads, preferred_element_type=jnp.float32)
        * 0.125
    )
    return jnp.where(allowed[None], scores, -1000000000.0)


def weight_terms(
    normed_one, grad_stack, attended, grad_attn, normed_two, grad_pre, gate_rows, grad_mlp
):
    term_qkv = jnp.einsum("ld,tlc->tdc", normed_one, grad_stack, preferred_element_type=jnp.float32)
    term_out = jnp.dot(attended.T, grad_attn, preferred_element_type=jnp.float32)
    term_fc = jnp.dot(normed_two.T, grad_pre, preferred_element_type=jnp.float32)
    term_proj = jnp.dot(gate_rows.T, grad_mlp, preferred_element_type=jnp.float32)
    return (term_qkv, term_out, term_fc, term_proj)


def local(
    tokens,
    cotangent,
    segments,
    w_qkv,
    w_out,
    w_fc,
    w_proj,
    vec_norm,
    vec_split,
    first_qkv,
    first_out,
    first_fc,
    first_proj,
    first_norm,
    first_split,
    second_qkv,
    second_out,
    second_fc,
    second_proj,
    second_norm,
    second_split,
):
    send_qkv = w_qkv.astype(jnp.bfloat16)
    send_out = w_out.astype(jnp.bfloat16)
    send_fc = w_fc.astype(jnp.bfloat16)
    send_proj = w_proj.astype(jnp.bfloat16)
    send_norm = vec_norm.astype(jnp.bfloat16)
    send_split = vec_split.astype(jnp.bfloat16)
    masters = (w_qkv, w_out, w_fc, w_proj, vec_norm, vec_split)
    local_width = w_qkv.shape[2]
    local_heads = local_width // HD
    length = tokens.shape[1]
    row_index = lax.broadcasted_iota(jnp.int32, (length, length), 0)
    col_index = lax.broadcasted_iota(jnp.int32, (length, length), 1)
    output_rows = []
    gradient_rows = []
    saved_rows = []
    norm_terms = []
    split_terms = []
    for batch_index in range(tokens.shape[0]):
        gathered = (
            lax.all_gather(send_qkv, "dp", axis=1, tiled=True),
            lax.all_gather(send_out, "dp", axis=1, tiled=True),
            lax.all_gather(send_fc, "dp", axis=0, tiled=True),
            lax.all_gather(send_proj, "dp", axis=1, tiled=True),
            lax.all_gather(send_norm, "dp", axis=1, tiled=True),
            lax.all_gather(send_split, "dp", axis=1, tiled=True),
        )
        mat_qkv, mat_out, mat_fc, mat_proj = (gathered[0], gathered[1], gathered[2], gathered[3])
        row_norm = gathered[4].astype(jnp.float32)
        row_split = gathered[5].astype(jnp.float32)
        hidden_bias = row_split[2:6].T.reshape(-1)
        inputs = tokens[batch_index].astype(jnp.float32)
        segment_ids = segments[batch_index]
        allowed = (segment_ids[:, None] == segment_ids[None, :]) & (col_index <= row_index)
        first_in, first_back = jax.vjp(layer_norm, inputs, row_norm[0], row_norm[1])
        normed_one = first_in.astype(jnp.bfloat16)
        query_rows = (
            jnp.dot(normed_one, mat_qkv[0], preferred_element_type=jnp.float32) + row_split[0]
        ).astype(jnp.bfloat16)
        key_rows = jnp.dot(normed_one, mat_qkv[1], preferred_element_type=jnp.float32).astype(
            jnp.bfloat16
        )
        value_rows = (
            jnp.dot(normed_one, mat_qkv[2], preferred_element_type=jnp.float32) + row_split[1]
        ).astype(jnp.bfloat16)
        query_heads = query_rows.reshape(length, local_heads, HD)
        key_heads = key_rows.reshape(length, local_heads, HD)
        value_heads = value_rows.reshape(length, local_heads, HD)
        scores = masked_scores(query_heads, key_heads, allowed)
        row_max = jnp.max(scores, axis=-1, keepdims=True)
        exponent = jnp.exp(scores - row_max)
        row_total = jnp.sum(exponent, axis=-1, keepdims=True)
        log_total = row_max + jnp.log(row_total)
        softmax_rows = (exponent / row_total).astype(jnp.bfloat16)
        attended = jnp.einsum(
            "hqk,khd->qhd", softmax_rows, value_heads, preferred_element_type=jnp.float32
        )
        attended = attended.reshape(length, local_width).astype(jnp.bfloat16)
        attn_part = jnp.dot(attended, mat_out, preferred_element_type=jnp.float32)
        attn_total = lax.psum(attn_part.astype(jnp.bfloat16), "mp").astype(jnp.float32)
        resid = inputs + attn_total + row_norm[4]
        second_in, second_back = jax.vjp(layer_norm, resid, row_norm[2], row_norm[3])
        normed_two = second_in.astype(jnp.bfloat16)
        pre_gate = jnp.dot(normed_two, mat_fc, preferred_element_type=jnp.float32) + hidden_bias
        gate_out, gate_back = jax.vjp(smooth_gate, pre_gate)
        gate_rows = gate_out.astype(jnp.bfloat16)
        mlp_part = jnp.dot(gate_rows, mat_proj, preferred_element_type=jnp.float32)
        mlp_total = lax.psum(mlp_part.astype(jnp.bfloat16), "mp").astype(jnp.float32)
        output_rows.append((resid + mlp_total + row_norm[5]).astype(jnp.bfloat16))
        fetched = (
            lax.all_gather(send_qkv, "dp", axis=1, tiled=True),
            lax.all_gather(send_out, "dp", axis=1, tiled=True),
            lax.all_gather(send_fc, "dp", axis=0, tiled=True),
            lax.all_gather(send_proj, "dp", axis=1, tiled=True),
        )
        back_qkv, back_out, back_fc, back_proj = (fetched[0], fetched[1], fetched[2], fetched[3])
        grad_top = cotangent[batch_index].astype(jnp.float32)
        grad_mlp = grad_top.astype(jnp.bfloat16)
        grad_gate = jnp.dot(grad_mlp, back_proj.T, preferred_element_type=jnp.float32)
        grad_pre = gate_back(grad_gate)[0].astype(jnp.bfloat16)
        grad_two_part = jnp.dot(grad_pre, back_fc.T, preferred_element_type=jnp.float32)
        grad_two = lax.psum(grad_two_part.astype(jnp.bfloat16), "mp").astype(jnp.float32)
        grad_resid_norm, grad_gain_two, grad_shift_two = second_back(grad_two)
        grad_resid = grad_top + grad_resid_norm
        grad_attn = grad_resid.astype(jnp.bfloat16)
        grad_heads = jnp.dot(grad_attn, back_out.T, preferred_element_type=jnp.float32).astype(
            jnp.bfloat16
        )
        grad_heads = grad_heads.reshape(length, local_heads, HD)
        again_scores = masked_scores(query_heads, key_heads, allowed)
        again_probs = jnp.exp(again_scores - log_total)
        grad_probs = jnp.einsum(
            "qhd,khd->hqk", grad_heads, value_heads, preferred_element_type=jnp.float32
        )
        grad_scores = again_probs * (
            grad_probs - jnp.sum(again_probs * grad_probs, axis=-1, keepdims=True)
        )
        grad_scores = grad_scores.astype(jnp.bfloat16)
        grad_query = (
            jnp.einsum("hqk,khd->qhd", grad_scores, key_heads, preferred_element_type=jnp.float32)
            * 0.125
        ).astype(jnp.bfloat16)
        grad_key = (
            jnp.einsum("hqk,qhd->khd", grad_scores, query_heads, preferred_element_type=jnp.float32)
            * 0.125
        ).astype(jnp.bfloat16)
        grad_value = jnp.einsum(
            "hqk,qhd->khd", softmax_rows, grad_heads, preferred_element_type=jnp.float32
        ).astype(jnp.bfloat16)
        grad_stack = jnp.stack(
            [
                grad_query.reshape(length, local_width),
                grad_key.reshape(length, local_width),
                grad_value.reshape(length, local_width),
            ]
        )
        grad_one_part = jnp.einsum(
            "tlc,tdc->ld", grad_stack, back_qkv, preferred_element_type=jnp.float32
        )
        grad_one = lax.psum(grad_one_part.astype(jnp.bfloat16), "mp").astype(jnp.float32)
        grad_input, grad_gain_one, grad_shift_one = first_back(grad_one)
        gradient_rows.append((grad_resid + grad_input).astype(jnp.bfloat16))
        term_norm = jnp.stack(
            [
                grad_gain_one,
                grad_shift_one,
                grad_gain_two,
                grad_shift_two,
                jnp.sum(grad_resid, axis=0),
                jnp.sum(grad_top, axis=0),
            ]
        )
        stack_sums = jnp.sum(grad_stack.astype(jnp.float32), axis=1)
        hidden_sums = jnp.sum(grad_pre.astype(jnp.float32), axis=0).reshape(local_width, 4).T
        term_split = jnp.concatenate([stack_sums[0:1], stack_sums[2:3], hidden_sums], axis=0)
        saved_rows.append(
            (normed_one, grad_stack, attended, grad_attn, normed_two, grad_pre, gate_rows, grad_mlp)
        )
        norm_terms.append(term_norm)
        split_terms.append(term_split)
    joined = [
        jnp.concatenate([saved[index] for saved in saved_rows], axis=1 if index == 1 else 0)
        for index in range(8)
    ]
    term_qkv, term_out, term_fc, term_proj = weight_terms(
        joined[0], joined[1], joined[2], joined[3], joined[4], joined[5], joined[6], joined[7]
    )
    sum_norm = norm_terms[0]
    sum_split = split_terms[0]
    sum_norm = sum_norm + norm_terms[1]
    sum_split = sum_split + split_terms[1]
    reduced = (
        lax.psum_scatter(term_qkv, "dp", scatter_dimension=1, tiled=True),
        lax.psum_scatter(term_out, "dp", scatter_dimension=1, tiled=True),
        lax.psum_scatter(term_fc, "dp", scatter_dimension=0, tiled=True),
        lax.psum_scatter(term_proj, "dp", scatter_dimension=1, tiled=True),
        lax.psum_scatter(sum_norm, "dp", scatter_dimension=1, tiled=True),
        lax.psum_scatter(sum_split, "dp", scatter_dimension=1, tiled=True),
    )
    firsts = (first_qkv, first_out, first_fc, first_proj, first_norm, first_split)
    seconds = (second_qkv, second_out, second_fc, second_proj, second_norm, second_split)
    rates = rate_list()
    decays = (0.1, 0.1, 0.1, 0.1, 0.0, 0.0)
    updated = [
        adamw(
            masters[index],
            reduced[index],
            firsts[index],
            seconds[index],
            rates[index],
            decays[index],
        )
        for index in range(6)
    ]
    out_tokens = jnp.stack(output_rows)
    in_grad = jnp.stack(gradient_rows)
    return (
        out_tokens,
        in_grad,
        updated[0][0],
        updated[1][0],
        updated[2][0],
        updated[3][0],
        updated[4][0],
        updated[5][0],
        updated[0][1],
        updated[1][1],
        updated[2][1],
        updated[3][1],
        updated[4][1],
        updated[5][1],
        updated[0][2],
        updated[1][2],
        updated[2][2],
        updated[3][2],
        updated[4][2],
        updated[5][2],
    )


def solution(mesh):
    return jax.shard_map(
        local,
        mesh=mesh,
        in_specs=(
            P(None, "dp", None),
            P(None, "dp", None),
            P(None, "dp"),
            P(None, "dp", "mp"),
            P("mp", "dp"),
            P("dp", "mp"),
            P("mp", "dp"),
            P(None, "dp"),
            P(None, ("mp", "dp")),
            P(None, "dp", "mp"),
            P("mp", "dp"),
            P("dp", "mp"),
            P("mp", "dp"),
            P(None, "dp"),
            P(None, ("mp", "dp")),
            P(None, "dp", "mp"),
            P("mp", "dp"),
            P("dp", "mp"),
            P("mp", "dp"),
            P(None, "dp"),
            P(None, ("mp", "dp")),
        ),
        out_specs=(
            P(None, "dp", None),
            P(None, "dp", None),
            P(None, "dp", "mp"),
            P("mp", "dp"),
            P("dp", "mp"),
            P("mp", "dp"),
            P(None, "dp"),
            P(None, ("mp", "dp")),
            P(None, "dp", "mp"),
            P("mp", "dp"),
            P("dp", "mp"),
            P("mp", "dp"),
            P(None, "dp"),
            P(None, ("mp", "dp")),
            P(None, "dp", "mp"),
            P("mp", "dp"),
            P("dp", "mp"),
            P("mp", "dp"),
            P(None, "dp"),
            P(None, ("mp", "dp")),
        ),
        check_vma=False,
    )
```

profile of v0, /device:TPU:0, one launch (start us, length us, event | category | flops | bytes accessed | tf_op | source)
XLA Modules:
  0.0 961.4 jit_solution(16590691971688995265)
XLA Ops:
  7.2 1.7 convert_element_type.264
  11.4 23.3 %all-gather.1 = bf16[16,32,6]{1,2,0:T(8,128)(2,1)S(1)} all-gather(bf16[1,32,6]{1,2,0:T(8,128)(2,1)S(1)} %convert_bitcast_fusion.2), channel_id=1, replica_groups=mesh['dp'=16,'mp'=2] {'dp'}, dimensions={0}, use_global_device_ids=true | all-gather | bytes 6528 | tf_op jit(solution)/shard_map/all_gather | solution.py:113
  35.4 17.8 %all-gather = bf16[16,64,6]{1,2,0:T(8,128)(2,1)S(1)} all-gather(bf16[1,64,6]{1,2,0:T(8,128)(2,1)S(1)} %convert_bitcast_fusion.3), channel_id=1, replica_groups=mesh['dp'=16,'mp'=2] {'dp'}, dimensions={0}, use_global_device_ids=true | all-gather | bytes 13056 | tf_op jit(solution)/shard_map/all_gather | solution.py:112
  57.1 2.0 all-gather.7.cloned.1.call-done
  60.8 1.7 fusion.13
  65.1 33.5 %all-gather.9.cloned.1.call-done = bf16[512,1024]{0,1:T(8,128)(2,1)} async-done(((bf16[512,64]{0,1:T(8,128)(2,1)}), bf16[512,1024]{0,1:T(8,128)(2,1)}) %all-gather.9.cloned.1.call-update) | async-done | bytes 1048592 | tf_op jit(solution)/shard_map/all_gather | solution.py:109
  98.6 2.3 convolution_convert_fusion.8
  101.0 20.8 %all-reduce.9.cloned.1.call-done = bf16[64,1024]{1,0:T(8,128)(2,1)} async-done(((bf16[64,1024]{1,0:T(8,128)(2,1)}), bf16[64,1024]{1,0:T(8,128)(2,1)}) %all-reduce.9.cloned.1.call-update) | async-done | bytes 131088 | tf_op jit(solution)/shard_map/psum | solution.py:147
  132.4 19.7 %all-reduce.11.cloned.1.call-done = bf16[64,1024]{1,0:T(8,128)(2,1)} async-done(((bf16[64,1024]{1,0:T(8,128)(2,1)}), bf16[64,1024]{1,0:T(8,128)(2,1)}) %all-reduce.11.cloned.1.call-update) | async-done | bytes 131088 | tf_op jit(solution)/shard_map/psum | solution.py:147
  155.5 49.9 %all-gather.11.cloned.1.call-done = bf16[1024,2048]{1,0:T(8,128)(2,1)} async-done(((bf16[64,2048]{1,0:T(8,128)(2,1)}), bf16[1024,2048]{1,0:T(8,128)(2,1)}) %all-gather.11.cloned.1.call-update) | async-done | bytes 4194320 | tf_op jit(solution)/shard_map/all_gather | solution.py:110
  205.4 4.1 multiply_convert_fusion
  209.5 1.7 multiply_convert_fusion.1
  211.3 4.5 fusion.36
  215.9 103.2 %reduce-scatter.14.cloned.1.call-done = f32[2048,64]{0,1:T(8,128)} async-done(((f32[2048,1024]{0,1:T(8,128)}), f32[2048,64]{0,1:T(8,128)}) %reduce-scatter.14.cloned.1.call-update) | async-done | bytes 524304 | tf_op jit(solution)/shard_map/reduce_scatter | solution.py:243
  319.1 3.2 multiply_subtract_fusion
  324.4 48.4 %all-gather.13.cloned.1.call-done = bf16[2048,1024]{0,1:T(8,128)(2,1)} async-done(((bf16[2048,64]{0,1:T(8,128)(2,1)}), bf16[2048,1024]{0,1:T(8,128)(2,1)}) %all-gather.13.cloned.1.call-update) | async-done | bytes 4194320 | tf_op jit(solution)/shard_map/all_gather | solution.py:111
  372.7 3.5 convert_reduce_fusion.1
  378.9 4.2 convert_reduce_fusion
  385.7 4.4 convolution_convert_fusion.1
  390.1 2.1 convolution_convert_fusion
  392.3 4.4 convolution_convert_fusion.2
  396.7 2.1 convolution_convert_fusion.3
  398.7 15.4 %all-reduce.17.cloned.1.call-done = (bf16[64,1024]{1,0:T(8,128)(2,1)}, bf16[64,1024]{1,0:T(8,128)(2,1)}) async-done(((bf16[64,1024]{1,0:T(8,128)(2,1)}, bf16[64,1024]{1,0:T(8,128)(2,1)}), (bf16[64,1024]{1,0:T(8,128)(2,1)}, bf16[64,1024]{1,0:T(8,128)(2,1)})) %all-reduce.17.cloned.1.call-update) | async-done | bytes 262160 | tf_op jit(solution)/shard_map/psum | solution.py:169
  414.1 1.8 fusion.77
  416.0 1.9 fusion.92
  417.9 1.9 fusion.159
  428.9 1.8 fusion.10
  430.7 1.8 fusion.11
  435.8 1.7 stack_reshape.22
  439.1 1.7 stack_reshape.21
  444.0 1.7 stack_reshape.19
  447.4 1.7 stack_reshape.18
  452.1 3.7 fusion.7
  455.9 2.6 fusion.6
  462.1 25.7 %all-reduce.15.cloned.1.call-done = (bf16[64,1024]{1,0:T(8,128)(2,1)}, bf16[64,1024]{1,0:T(8,128)(2,1)}, bf16[64,1024]{1,0:T(8,128)(2,1)}, bf16[64,1024]{1,0:T(8,128)(2,1)}) async-done(((bf16[64,1024]{1,0:T(8,128)(2,1)}, bf16[64,1024]{1,0:T(8,128)(2,1)}, bf16[64,1024]{1,0:T(8,128)(2,1)}, bf16[64,1024]{1,0:T(8,128)(2,1)}), (bf16[64,1024]{1,0:T(8,128)(2,1)}, bf16[64,1024]{1,0:T(8,128)(2,1)}, ...) | async-done | bytes 524304 | tf_op jit(solution)/shard_map/psum | solution.py:155
  490.7 2.1 fusion.73
  495.5 1.9 fusion.98
  497.6 3.7 convolution_bitcast_fusion
  501.3 9.5 copy.265
  512.0 4.5 fusion.32
  518.4 28.7 %reduce-scatter.18.cloned.1.call-done = f32[32,6]{1,0:T(8,128)} async-done(((f32[512,6]{1,0:T(8,128)}), f32[32,6]{1,0:T(8,128)}) %reduce-scatter.18.cloned.1.call-update) | async-done | bytes 784
  553.0 53.1 %reduce-scatter.16.cloned.1.call-done = f32[64,6]{1,0:T(8,128)} async-done(((f32[1024,6]{1,0:T(8,128)}), f32[64,6]{1,0:T(8,128)}) %reduce-scatter.16.cloned.1.call-update) | async-done | bytes 1552
  608.3 62.5 %reduce-scatter.10.cloned.1.call-done = f32[512,64]{0,1:T(8,128)} async-done(((f32[512,1024]{0,1:T(8,128)}), f32[512,64]{0,1:T(8,128)}) %reduce-scatter.10.cloned.1.call-update) | async-done | bytes 131088 | tf_op jit(solution)/shard_map/reduce_scatter | solution.py:241
  670.8 1.8 multiply_subtract_fusion.3
  672.5 170.9 %all-reduce.13.cloned.1.call-done = f32[3,1024,512]{2,0,1:T(4,128)} async-done(((f32[3,1024,512]{2,0,1:T(4,128)}), f32[3,1024,512]{2,0,1:T(4,128)}) %all-reduce.13.cloned.1.call-update) | async-done | bytes 6291472
  844.6 2.4 multiply_subtract_fusion.2
  847.0 105.4 %reduce-scatter.12.cloned.1.call-done = f32[64,2048]{1,0:T(8,128)} async-done(((f32[1024,2048]{1,0:T(8,128)}), f32[64,2048]{1,0:T(8,128)}) %reduce-scatter.12.cloned.1.call-update) | async-done | bytes 524304 | tf_op jit(solution)/shard_map/reduce_scatter | solution.py:242
  952.4 2.4 multiply_subtract_fusion.1
  (305 shorter events, 75.0 us)
Async XLA Ops:
  7.2 55.5 %copy-start.2 = (bf16[2,64,1024]{2,1,0:T(8,128)(2,1)S(1)}, bf16[2,64,1024]{2,1,0:T(8,128)(2,1)}, u32[]{:S(2)}) copy-start(bf16[2,64,1024]{2,1,0:T(8,128)(2,1)} %param.21) | copy-start | bytes 786436
  7.2 51.8 %all-gather.7.cloned.1.call-start = ((), (), s32[]{:S(2)}) async-start(), calls=%async_computation.5 | async-start | bytes 3342336 | tf_op jit(solution)/shard_map/all_gather | solution.py:108
  9.0 89.6 %all-gather.9.cloned.1.call-start = ((), (), s32[]{:S(2)}) async-start(), calls=%async_computation.6 | async-start | bytes 1114112 | tf_op jit(solution)/shard_map/all_gather | solution.py:109
  10.6 111.2 %all-reduce.9.cloned.1.call-start = ((), (), s32[]{:S(2)}) async-start(), calls=%async_computation.7 | async-start | bytes 262144 | tf_op jit(solution)/shard_map/psum | solution.py:147
  57.0 69.9 %copy-start.49 = (f32[1,1024]{1,0:T(1,128)}, f32[1,1024]{1,0:T(1,128)S(1)}, u32[]{:S(2)}) copy-start(f32[1,1024]{1,0:T(1,128)S(1)} %get-tuple-element.180) | copy-start | bytes 12292
  57.1 69.9 %copy-start.57 = (f32[1,1024]{1,0:T(1,128)}, f32[1,1024]{1,0:T(1,128)S(1)}, u32[]{:S(2)}) copy-start(f32[1,1024]{1,0:T(1,128)S(1)} %get-tuple-element.179) | copy-start | bytes 12292
  60.8 37.8 %copy-start.46 = (bf16[64,8,64]{2,1,0:T(8,128)(2,1)}, bf16[64,8,64]{2,1,0:T(8,128)(2,1)S(1)}, u32[]{:S(2)}) copy-start(bf16[64,8,64]{2,1,0:T(8,128)(2,1)S(1)} %reshape.470) | copy-start | bytes 196612
  62.7 35.9 %copy-start.25 = (bf16[64,512]{0,1:T(8,128)(2,1)}, bf16[64,512]{0,1:T(8,128)(2,1)S(1)}, u32[]{:S(2)}) copy-start(bf16[64,512]{0,1:T(8,128)(2,1)S(1)} %copy.289) | copy-start | bytes 196612
  64.7 58.7 %copy-start.51 = (f32[8,64]{1,0:T(8,128)}, f32[8,64]{1,0:T(8,128)S(1)}, u32[]{:S(2)}) copy-start(f32[8,64]{1,0:T(8,128)S(1)} %get-tuple-element.189) | copy-start | bytes 6148
  64.7 360.2 %copy-start.8 = (f32[8,64,64]{1,2,0:T(8,128)}, f32[8,64,64]{1,2,0:T(8,128)S(1)}, u32[]{:S(2)}) copy-start(f32[8,64,64]{1,2,0:T(8,128)S(1)} %get-tuple-element.190) | copy-start | bytes 393220
  64.8 63.8 %copy-start.58 = (f32[8,64]{1,0:T(8,128)}, f32[8,64]{1,0:T(8,128)S(1)}, u32[]{:S(2)}) copy-start(f32[8,64]{1,0:T(8,128)S(1)} %fusion.108) | copy-start | bytes 6148
  101.0 51.1 %all-reduce.11.cloned.1.call-start = ((), (), s32[]{:S(2)}) async-start(), calls=%async_computation.10 | async-start | bytes 262144 | tf_op jit(solution)/shard_map/psum | solution.py:147
  130.5 74.9 %all-gather.11.cloned.1.call-start = ((), (), s32[]{:S(2)}) async-start(), calls=%async_computation.8 | async-start | bytes 4456448 | tf_op jit(solution)/shard_map/all_gather | solution.py:110
  131.3 187.8 %reduce-scatter.14.cloned.1.call-start = ((), (), s32[]{:S(2)}) async-start(), calls=%async_computation.13 | async-start | bytes 8912896 | tf_op jit(solution)/shard_map/reduce_scatter | solution.py:243
  132.4 77.1 %copy-start.66 = (f32[64]{0:T(128)}, f32[64]{0:T(128)S(1)}, u32[]{:S(2)}) copy-start(f32[64]{0:T(128)S(1)} %broadcast_multiply_fusion.2) | copy-start | bytes 772
  153.2 56.3 %copy-start.68 = (f32[64]{0:T(128)}, f32[64]{0:T(128)S(1)}, u32[]{:S(2)}) copy-start(f32[64]{0:T(128)S(1)} %broadcast_multiply_fusion) | copy-start | bytes 772
  154.3 55.2 %copy-start.84 = (f32[64]{0:T(128)}, f32[64]{0:T(128)S(1)}, u32[]{:S(2)}) copy-start(f32[64]{0:T(128)S(1)} %multiply_reduce_fusion.2) | copy-start | bytes 772
  154.4 55.1 %copy-start.72 = (f32[64]{0:T(128)}, f32[64]{0:T(128)S(1)}, u32[]{:S(2)}) copy-start(f32[64]{0:T(128)S(1)} %fusion.137) | copy-start | bytes 772
  154.4 55.1 %copy-start.74 = (f32[64]{0:T(128)}, f32[64]{0:T(128)S(1)}, u32[]{:S(2)}) copy-start(f32[64]{0:T(128)S(1)} %fusion.139) | copy-start | bytes 772
  155.5 54.0 %copy-start.19 = (bf16[64,1024]{1,0:T(8,128)(2,1)}, bf16[64,1024]{1,0:T(8,128)(2,1)S(1)}, u32[]{:S(2)}) copy-start(bf16[64,1024]{1,0:T(8,128)(2,1)S(1)} %get-tuple-element.160) | copy-start | bytes 393220
  155.5 55.8 %copy-start.17 = (bf16[64,1024]{1,0:T(8,128)(2,1)}, bf16[64,1024]{1,0:T(8,128)(2,1)S(1)}, u32[]{:S(2)}) copy-start(bf16[64,1024]{1,0:T(8,128)(2,1)S(1)} %get-tuple-element.159) | copy-start | bytes 393220
  215.8 107.3 %copy-start.52 = (f32[8,64]{1,0:T(8,128)S(1)}, f32[8,64]{1,0:T(8,128)}, u32[]{:S(2)}) copy-start(f32[8,64]{1,0:T(8,128)} %copy-done.51) | copy-start | bytes 6148
  215.8 107.3 %copy-start.59 = (f32[8,64]{1,0:T(8,128)S(1)}, f32[8,64]{1,0:T(8,128)}, u32[]{:S(2)}) copy-start(f32[8,64]{1,0:T(8,128)} %copy-done.58) | copy-start | bytes 6148
  215.9 107.9 %copy-start.54 = (f32[8,64]{1,0:T(8,128)S(1)}, f32[8,64]{1,0:T(8,128)}, u32[]{:S(2)}) copy-start(f32[8,64]{1,0:T(8,128)} %copy-done.53) | copy-start | bytes 6148
  215.9 107.9 %copy-start.62 = (f32[8,64]{1,0:T(8,128)S(1)}, f32[8,64]{1,0:T(8,128)}, u32[]{:S(2)}) copy-start(f32[8,64]{1,0:T(8,128)} %copy-done.61) | copy-start | bytes 6148
  215.9 156.9 %all-gather.13.cloned.1.call-start = ((), (), s32[]{:S(2)}) async-start(), calls=%async_computation.9 | async-start | bytes 4456448 | tf_op jit(solution)/shard_map/all_gather | solution.py:111
  322.3 91.9 %all-reduce.17.cloned.1.call-start = ((), (), s32[]{:S(2)}) async-start(), calls=%async_computation.18 | async-start | bytes 524288 | tf_op jit(solution)/shard_map/psum | solution.py:169
  392.2 95.6 %all-reduce.15.cloned.1.call-start = ((), (), s32[]{:S(2)}) async-start(), calls=%async_computation.17 | async-start | bytes 1048576 | tf_op jit(solution)/shard_map/psum | solution.py:155
  450.6 37.2 %copy-start.50 = (f32[1,1024]{1,0:T(1,128)S(1)}, f32[1,1024]{1,0:T(1,128)}, u32[]{:S(2)}) copy-start(f32[1,1024]{1,0:T(1,128)} %copy-done.49) | copy-start | bytes 12292
  458.5 37.0 %copy-start.22 = (bf16[64,1024]{1,0:T(8,128)(2,1)S(1)}, bf16[64,1024]{1,0:T(8,128)(2,1)}, u32[]{:S(2)}) copy-start(bf16[64,1024]{1,0:T(8,128)(2,1)} %copy-done.21) | copy-start | bytes 393220
  458.5 37.0 %copy-start.24 = (bf16[64,1024]{1,0:T(8,128)(2,1)S(1)}, bf16[64,1024]{1,0:T(8,128)(2,1)}, u32[]{:S(2)}) copy-start(bf16[64,1024]{1,0:T(8,128)(2,1)} %copy-done.23) | copy-start | bytes 393220
  458.5 37.0 %copy-start.42 = (bf16[8,64,64]{2,1,0:T(8,128)(2,1)S(1)}, bf16[8,64,64]{2,1,0:T(8,128)(2,1)}, u32[]{:S(2)}) copy-start(bf16[8,64,64]{2,1,0:T(8,128)(2,1)} %copy-done.41) | copy-start | bytes 196612
  458.5 37.0 %copy-start.44 = (bf16[8,64,64]{2,1,0:T(8,128)(2,1)S(1)}, bf16[8,64,64]{2,1,0:T(8,128)(2,1)}, u32[]{:S(2)}) copy-start(bf16[8,64,64]{2,1,0:T(8,128)(2,1)} %copy-done.43) | copy-start | bytes 196612
  458.5 88.6 %reduce-scatter.18.cloned.1.call-start = ((), (), s32[]{:S(2)}) async-start(), calls=%async_computation.15 | async-start | bytes 278528
  461.8 35.8 %copy-start.32 = (bf16[1,64,512]{2,1,0:T(8,128)(2,1)S(1)}, bf16[1,64,512]{2,1,0:T(8,128)(2,1)}, u32[]{:S(2)}) copy-start(bf16[1,64,512]{2,1,0:T(8,128)(2,1)} %copy.250) | copy-start | bytes 196612
  461.8 35.8 %copy-start.33 = (bf16[1,64,512]{2,1,0:T(8,128)(2,1)S(1)}, bf16[1,64,512]{2,1,0:T(8,128)(2,1)}, u32[]{:S(2)}) copy-start(bf16[1,64,512]{2,1,0:T(8,128)(2,1)} %stack_reshape.19) | copy-start | bytes 196612
  461.8 35.8 %copy-start.34 = (bf16[1,64,512]{2,1,0:T(8,128)(2,1)S(1)}, bf16[1,64,512]{2,1,0:T(8,128)(2,1)}, u32[]{:S(2)}) copy-start(bf16[1,64,512]{2,1,0:T(8,128)(2,1)} %stack_reshape.18) | copy-start | bytes 196612
  461.8 144.3 %reduce-scatter.16.cloned.1.call-start = ((), (), s32[]{:S(2)}) async-start(), calls=%async_computation.14 | async-start | bytes 557056
  495.4 175.3 %reduce-scatter.10.cloned.1.call-start = ((), (), s32[]{:S(2)}) async-start(), calls=%async_computation.11 | async-start | bytes 2228224 | tf_op jit(solution)/shard_map/reduce_scatter | solution.py:241
  497.5 346.0 %all-reduce.13.cloned.1.call-start = ((), (), s32[]{:S(2)}) async-start(), calls=%async_computation.16 | async-start | bytes 16777216
  510.9 441.5 %reduce-scatter.12.cloned.1.call-start = ((), (), s32[]{:S(2)}) async-start(), calls=%async_computation.12 | async-start | bytes 8912896 | tf_op jit(solution)/shard_map/reduce_scatter | solution.py:242
  516.6 90.4 %copy-start.65 = (f32[6,64]{1,0:T(8,128)S(1)}, f32[6,64]{1,0:T(8,128)}, u32[]{:S(2)}) copy-start(f32[6,64]{1,0:T(8,128)} %param.28) | copy-start | bytes 4612
  516.6 154.2 %copy-start.45 = (f32[512,64]{0,1:T(8,128)S(1)}, f32[512,64]{0,1:T(8,128)}, u32[]{:S(2)}) copy-start(f32[512,64]{0,1:T(8,128)} %param.25) | copy-start | bytes 393220
  516.6 154.2 %copy-start.48 = (f32[512,64]{0,1:T(8,128)S(1)}, f32[512,64]{0,1:T(8,128)}, u32[]{:S(2)}) copy-start(f32[512,64]{0,1:T(8,128)} %param.31) | copy-start | bytes 393220
  516.6 328.0 %copy-start.16 = (f32[3,64,512]{2,1,0:T(8,128)S(1)}, f32[3,64,512]{2,1,0:T(8,128)}, u32[]{:S(2)}) copy-start(f32[3,64,512]{2,1,0:T(8,128)} %param.24) | copy-start | bytes 1179652
  516.6 435.8 %copy-start.15 = (f32[64,2048]{1,0:T(8,128)S(1)}, f32[64,2048]{1,0:T(8,128)}, u32[]{:S(2)}) copy-start(f32[64,2048]{1,0:T(8,128)} %param.26) | copy-start | bytes 1572868
  516.6 435.8 %copy-start.39 = (f32[64,2048]{1,0:T(8,128)S(1)}, f32[64,2048]{1,0:T(8,128)}, u32[]{:S(2)}) copy-start(f32[64,2048]{1,0:T(8,128)} %param.32) | copy-start | bytes 1572868
  516.7 435.8 %copy-start.40 = (f32[64,2048]{1,0:T(8,128)S(1)}, f32[64,2048]{1,0:T(8,128)}, u32[]{:S(2)}) copy-start(f32[64,2048]{1,0:T(8,128)} %param.38) | copy-start | bytes 1572868
  (53 other events, 802.5 us)
Sparse Core Ops, SparseCore 0:
  10.8 48.2 all-gather.6
  61.8 36.7 all-gather.8
  101.4 20.3 all-reduce.8
  130.6 21.4 all-reduce.10
  154.6 50.7 all-gather.10
  216.0 103.1 reduce-scatter.13
  322.4 50.2 all-gather.12
  392.2 21.8 all-reduce.16
  458.6 29.1 all-reduce.14
  491.8 55.2 reduce-scatter.17
  551.2 54.8 reduce-scatter.15
  610.1 60.5 reduce-scatter.9
  674.5 168.8 all-reduce.12
  847.9 104.4 reduce-scatter.11
where the time goes:
time: 963 us; the launch traced here: 961 us
  waiting for transfers between devices  739 us (77%)
  matrix products  71.4 us (7%)
  other arithmetic  47.6 us (5%)
  local copies, waits for them, and re-layouts  45.1 us (5%)
  blocking collectives  41.1 us (4%)
  between operations  15.8 us (2%)
    unnamed x17, waiting for transfers between devices  253 us
    reduce_scatter x1, waiting for transfers between devices, local(): lax.psum_scatter(term_fc, 'dp', scatter_dimension=0, tiled=True)  105 us
    reduce_scatter x1, waiting for transfers between devices, local(): lax.psum_scatter(term_proj, 'dp', scatter_dimension=1, tiled=True)  103 us
    reduce_scatter x1, waiting for transfers between devices, local(): lax.psum_scatter(term_out, 'dp', scatter_dimension=1, tiled=True)  62.5 us
    all_gather x1, waiting for transfers between devices, local(): lax.all_gather(send_fc, 'dp', axis=0, tiled=True)  49.9 us
    all_gather x1, waiting for transfers between devices, local(): lax.all_gather(send_proj, 'dp', axis=1, tiled=True)  48.4 us
    psum x2, waiting for transfers between devices, local(): lax.psum(attn_part.astype(jnp.bfloat16), 'mp').astype(jnp.float32)  40.4 us
    all_gather x1, waiting for transfers between devices, local(): lax.all_gather(send_out, 'dp', axis=1, tiled=True)  33.5 us
  transfers between devices with their start and end apart: 14, of which 14 were waited for; matrix products, arithmetic and copies ran while one was open for 7% of the time, Pallas kernels for 0%

commit v1 on v0

v1 whole, which is shorter than its diff:
```python
import functools
import math

import jax
import jax.numpy as jnp
from jax import lax
from jax.experimental import pallas as pl
from jax.experimental.pallas import tpu as pltpu
from jax.sharding import PartitionSpec as P

D = 1024
HD = 64
FF = 4096
TOK_MB = 64
STEP = 10
BF = jnp.bfloat16
F32 = jnp.float32
EXT = 16
VMEM_LIMIT = 60 * 1024 * 1024

NN = (((1,), (0,)), ((), ()))
NT = (((1,), (1,)), ((), ()))
TN = (((0,), (0,)), ((), ()))


def dot(a, b, dims=NN):
    return lax.dot_general(a, b, dims, preferred_element_type=F32)


def rate_list():
    narrow = D // min(32, max(2, TOK_MB // 4))
    return (
        2.0 / math.sqrt(D),
        2.0 / math.sqrt(narrow),
        2.0 / math.sqrt(D),
        2.0 / math.sqrt(FF),
        0.8,
        0.4,
    )


def adamw(weight, gradient, first_moment, second, step_rate, weight_decay):
    first_new = 0.9 * first_moment + 0.1 * gradient
    second_new = 0.95 * second + 0.05 * gradient * gradient
    scaled_first = first_new / (1.0 - 0.9**STEP)
    scaled_second = second_new / (1.0 - 0.95**STEP)
    weight_new = weight - step_rate * (
        scaled_first / (jnp.sqrt(scaled_second) + 1e-08) + weight_decay * weight
    )
    return (weight_new, first_new, second_new)


def make_parts(widths):
    qkv, out, fc, proj, ext = widths
    half_fc, half_proj = fc // 2, proj // 2
    return (
        (0, 0, qkv, 0),
        (2, half_fc, half_fc, 1),
        (1, 0, out, 0),
        (3, 0, half_proj, 1),
        (2, 0, half_fc, 0),
        (3, half_proj, half_proj, 1),
        (4, 0, ext, 1),
    )


def chip_at(position, chips):
    half = chips // 2
    high = lax.div(position, half)
    return (1 - high) * 2 * position + high * (2 * (chips - 1 - position) + 1)


def position_of(chip, chips):
    odd = lax.rem(chip, 2)
    row = lax.div(chip, 2)
    return (1 - odd) * row + odd * (chips - 1 - row)


def ring_place(chips):
    me = lax.axis_index("dp")
    core = lax.rem(me, 2)
    place = position_of(lax.div(me, 2), chips)

    def device(position):
        return chip_at(lax.rem(position + 2 * chips, chips), chips) * 2 + core

    return me, me + 1 - 2 * core, place, device


def greet(others):
    barrier = pltpu.get_barrier_semaphore()
    for other in others:
        pl.semaphore_signal(
            barrier, inc=1, device_id=other, device_id_type=pl.DeviceIdType.MESH
        )
    pl.semaphore_wait(barrier, len(others))


def remote(src, dst, send, recv, target):
    return pltpu.make_async_remote_copy(
        src_ref=src,
        dst_ref=dst,
        send_sem=send,
        recv_sem=recv,
        device_id={"dp": target},
        device_id_type=pl.DeviceIdType.MESH,
    )


def gather_kernel(chips, parts, *refs):
    ins, outs = refs[:5], refs[5:10]
    ring_send, ring_recv, side_send, side_recv = refs[10:]
    me, sibling, place, device = ring_place(chips)
    neighbours = (device(place + 1), device(place - 1))
    greet([{"dp": neighbours[0]}, {"dp": neighbours[1]}, {"dp": sibling}])
    for index in range(5):
        outs[index][me] = ins[index][...]

    def ring_copy(k, step):
        index, first, wide, way = parts[k]
        owner = device(place - step if way == 0 else place + step)
        block = outs[index].at[owner, :, pl.ds(first, wide)]
        return remote(
            block, block, ring_send.at[k, step], ring_recv.at[k, step], neighbours[way]
        )

    def side_copy(k, step):
        index, first, wide, way = parts[k]
        owner = device(place - step if way == 0 else place + step)
        block = outs[index].at[owner, :, pl.ds(first, wide)]
        return remote(block, block, side_send.at[k, step], side_recv.at[k, step], sibling)

    for k in range(len(parts)):
        ring_copy(k, 0).start()
    for k in range(len(parts)):
        side_copy(k, 0).start()

    @pl.loop(1, chips - 1)
    def _(step):
        for k in range(len(parts)):
            ring_copy(k, step - 1).wait_recv()
            ring_copy(k, step).start()
            side_copy(k, step).start()

    for k in range(len(parts)):
        ring_copy(k, chips - 2).wait_recv()
        side_copy(k, chips - 1).start()

    @pl.loop(0, chips - 1)
    def _(step):
        for k in range(len(parts)):
            ring_copy(k, step).wait_send()

    @pl.loop(0, chips)
    def _(step):
        for k in range(len(parts)):
            side_copy(k, step).wait()


def gather(blocks, count):
    chips = count // 2
    parts = make_parts([block.shape[1] for block in blocks])
    sems = [
        pltpu.SemaphoreType.DMA((len(parts), chips - 1)),
        pltpu.SemaphoreType.DMA((len(parts), chips - 1)),
        pltpu.SemaphoreType.DMA((len(parts), chips)),
        pltpu.SemaphoreType.DMA((len(parts), chips)),
    ]
    return pl.pallas_call(
        functools.partial(gather_kernel, chips, parts),
        out_shape=[jax.ShapeDtypeStruct((count,) + b.shape, b.dtype) for b in blocks],
        in_specs=[pl.BlockSpec(memory_space=pltpu.VMEM)] * 5,
        out_specs=[pl.BlockSpec(memory_space=pltpu.VMEM)] * 5,
        scratch_shapes=sems,
        compiler_params=pltpu.CompilerParams(
            collective_id=0, has_side_effects=True, vmem_limit_bytes=VMEM_LIMIT
        ),
        name="gather_weights",
    )(*blocks)


def reduce_kernel(chips, parts, *refs):
    lhs, rhs, ext = refs[:4], refs[4:8], refs[8]
    outs = refs[9:14]
    bufs = refs[14:19]
    terms = refs[19:24]
    left, right = refs[24:28], refs[28:32]
    ext_other = refs[32]
    ring_send, ring_recv, side_send, side_recv, local_sem = refs[33:]
    tokens = rhs[0].shape[0]
    me, sibling, place, device = ring_place(chips)
    neighbours = (device(place + 1), device(place - 1))
    greet([{"dp": neighbours[0]}, {"dp": neighbours[1]}, {"dp": sibling}])
    sides = []
    locals_ = []
    for m in range(4):
        sides.append(
            remote(
                lhs[m],
                left[m].at[:, :, pl.ds(tokens, tokens)],
                side_send.at[2 * m],
                side_recv.at[2 * m],
                sibling,
            )
        )
        sides.append(
            remote(
                rhs[m],
                right[m].at[pl.ds(tokens, tokens)],
                side_send.at[2 * m + 1],
                side_recv.at[2 * m + 1],
                sibling,
            )
        )
        locals_.append(
            pltpu.make_async_copy(
                lhs[m], left[m].at[:, :, pl.ds(0, tokens)], local_sem.at[2 * m]
            )
        )
        locals_.append(
            pltpu.make_async_copy(
                rhs[m], right[m].at[pl.ds(0, tokens)], local_sem.at[2 * m + 1]
            )
        )
    sides.append(remote(ext, ext_other, side_send.at[8], side_recv.at[8], sibling))
    for copy in sides:
        copy.start()
    for copy in locals_:
        copy.start()
    for copy in sides:
        copy.wait()
    for copy in locals_:
        copy.wait()

    def owner_of(k, step):
        way = parts[k][3]
        return device(place - 1 - step if way == 0 else place + 1 + step)

    def term(k, step):
        index, first, wide, _ = parts[k]
        owner = owner_of(k, step)
        if index == 4:
            return ext[owner] + ext_other[owner]
        return dot(left[index][owner], right[index][:, pl.ds(first, wide)])

    def ring_copy(k, step):
        index, first, wide, way = parts[k]
        columns = pl.ds(first, wide)
        return remote(
            bufs[index].at[step, :, columns],
            bufs[index].at[step + 1, :, columns],
            ring_send.at[k, step],
            ring_recv.at[k, step],
            neighbours[way],
        )

    for k in range(len(parts)):
        index, first, wide, _ = parts[k]
        bufs[index][0, :, pl.ds(first, wide)] = term(k, 0).astype(BF)
        ring_copy(k, 0).start()

    def fill(step):
        for k in range(len(parts)):
            index, first, wide, _ = parts[k]
            terms[index][:, pl.ds(first, wide)] = term(k, step)

    @pl.loop(1, chips - 1)
    def _(step):
        fill(step)
        for k in range(len(parts)):
            index, first, wide, _ = parts[k]
            columns = pl.ds(first, wide)
            ring_copy(k, step - 1).wait_recv()
            bufs[index][step, :, columns] = (
                bufs[index][step, :, columns].astype(F32) + terms[index][:, columns]
            ).astype(BF)
            ring_copy(k, step).start()

    fill(chips - 1)
    for k in range(len(parts)):
        index, first, wide, _ = parts[k]
        columns = pl.ds(first, wide)
        ring_copy(k, chips - 2).wait_recv()
        outs[index][:, columns] = (
            bufs[index][chips - 1, :, columns].astype(F32) + terms[index][:, columns]
        )

    @pl.loop(0, chips - 1)
    def _(step):
        for k in range(len(parts)):
            ring_copy(k, step).wait_send()


def reduce_scatter(lhs, rhs, ext):
    count, rows, tokens = lhs[0].shape
    chips = count // 2
    widths = [r.shape[1] for r in rhs] + [ext.shape[2]]
    heights = [rows] * 4 + [ext.shape[1]]
    parts = make_parts(widths)
    scratch = [pltpu.VMEM((chips, h, w), BF) for h, w in zip(heights, widths)]
    scratch += [pltpu.VMEM((h, w), F32) for h, w in zip(heights, widths)]
    scratch += [pltpu.VMEM((count, rows, 2 * tokens), BF) for _ in range(4)]
    scratch += [pltpu.VMEM((2 * tokens, w), BF) for w in widths[:4]]
    scratch += [pltpu.VMEM(ext.shape, F32)]
    scratch += [
        pltpu.SemaphoreType.DMA((len(parts), chips - 1)),
        pltpu.SemaphoreType.DMA((len(parts), chips - 1)),
        pltpu.SemaphoreType.DMA((9,)),
        pltpu.SemaphoreType.DMA((9,)),
        pltpu.SemaphoreType.DMA((8,)),
    ]
    return pl.pallas_call(
        functools.partial(reduce_kernel, chips, parts),
        out_shape=[jax.ShapeDtypeStruct((h, w), F32) for h, w in zip(heights, widths)],
        in_specs=[pl.BlockSpec(memory_space=pltpu.VMEM)] * 9,
        out_specs=[pl.BlockSpec(memory_space=pltpu.VMEM)] * 5,
        scratch_shapes=scratch,
        compiler_params=pltpu.CompilerParams(
            collective_id=1, has_side_effects=True, vmem_limit_bytes=VMEM_LIMIT
        ),
        name="reduce_gradients",
    )(*lhs, *rhs, ext)


def normalize(values):
    center = values - jnp.mean(values, axis=-1, keepdims=True)
    spread = jnp.mean(center * center, axis=-1, keepdims=True)
    scale = lax.rsqrt(spread + 1e-05)
    return center * scale, scale


def normalize_back(grad, gain, unit, scale):
    inner = grad * gain
    return scale * (
        inner
        - jnp.mean(inner, axis=-1, keepdims=True)
        - unit * jnp.mean(inner * unit, axis=-1, keepdims=True)
    )


def head_mask(shape, which):
    lane = lax.broadcasted_iota(jnp.int32, shape, 1)
    return lax.div(lane, HD) == which


def head_probs(query, key, which, allowed):
    only = jnp.where(head_mask(query.shape, which), query, jnp.zeros_like(query))
    scores = jnp.where(allowed, dot(only, key, NT) * 0.125, -1000000000.0)
    exponent = jnp.exp(scores - jnp.max(scores, axis=-1, keepdims=True))
    return exponent / jnp.sum(exponent, axis=-1, keepdims=True)


def attend_body(tokens, allow, norm, split, w_qkv, w_out, a1, qkv, o, part):
    width = o.shape[1]
    unit, _ = normalize(tokens[...].astype(F32))
    a1[...] = (unit * norm[0:1] + norm[1:2]).astype(BF)
    for t in range(3):
        columns = pl.ds(t * width, width)
        rows = dot(a1[...], w_qkv[:, columns])
        if t != 1:
            rows = rows + split[pl.ds(t // 2, 1)]
        qkv[:, columns] = rows.astype(BF)
    allowed = allow[...] > 0.5
    for pair in range(width // (2 * HD)):
        first = pair * 2 * HD
        query, key, value = (
            qkv[:, pl.ds(t * width + first, 2 * HD)] for t in range(3)
        )
        total = jnp.zeros(query.shape, F32)
        for which in range(2):
            probs = head_probs(query, key, which, allowed).astype(BF)
            only = jnp.where(head_mask(value.shape, which), value, jnp.zeros_like(value))
            total = total + dot(probs, only)
        o[:, pl.ds(first, 2 * HD)] = total.astype(BF)
    part[...] = dot(o[...], w_out[...], NT).astype(BF)


def feed_body(
    tokens, mine, other, cot, norm, bias, w_fc, w_proj, r, a2, gl, dz, part
):
    rows = tokens[...].astype(F32) + (mine[...].astype(F32) + other[...].astype(F32))
    rows = rows + norm[4:5]
    r[...] = rows
    unit, _ = normalize(rows)
    a2[...] = (unit * norm[2:3] + norm[3:4]).astype(BF)
    width = gl.shape[1]
    step = 512
    root = math.sqrt(2.0 / math.pi)
    for first in range(0, width, step):
        columns = pl.ds(first, step)
        z = dot(a2[...], w_fc[:, columns]) + bias[:, columns]
        bent = jnp.tanh(root * (z + 0.044715 * z * z * z))
        gl[:, columns] = (0.5 * z * (1.0 + bent)).astype(BF)
        slope = 0.5 * (1.0 + bent) + 0.5 * z * (1.0 - bent * bent) * root * (
            1.0 + 3.0 * 0.044715 * z * z
        )
        dz[:, columns] = (slope * dot(cot[...], w_proj[:, columns])).astype(BF)
    part[:, pl.ds(0, D)] = dot(gl[...], w_proj[...], NT).astype(BF)
    part[:, pl.ds(D, D)] = dot(dz[...], w_fc[...], NT).astype(BF)


def back_body(
    mine, other, r, cot, allow, norm, qkv, w_out, w_qkv, out, dr, dao, dqkv, part, sums
):
    total = mine[...].astype(F32) + other[...].astype(F32)
    rows = r[...]
    out[...] = (rows + total[:, :D] + norm[5:6]).astype(BF)
    da2 = total[:, D:]
    unit, scale = normalize(rows)
    top = cot[...].astype(F32)
    grad = top + normalize_back(da2, norm[2:3], unit, scale)
    dr[...] = grad
    dao[...] = grad.astype(BF)
    sums[0:1] = jnp.sum(da2 * unit, axis=0, keepdims=True)
    sums[1:2] = jnp.sum(da2, axis=0, keepdims=True)
    sums[2:3] = jnp.sum(grad, axis=0, keepdims=True)
    sums[3:4] = jnp.sum(top, axis=0, keepdims=True)
    sums[4:8] = jnp.zeros((4, D), F32)
    width = w_out.shape[1]
    heads = dot(dao[...], w_out[...]).astype(BF)
    allowed = allow[...] > 0.5
    for pair in range(width // (2 * HD)):
        first = pair * 2 * HD
        query, key, value = (
            qkv[:, pl.ds(t * width + first, 2 * HD)] for t in range(3)
        )
        do = heads[:, first : first + 2 * HD]
        zero = jnp.zeros_like(query)
        dq = jnp.zeros(query.shape, F32)
        dk = jnp.zeros(query.shape, F32)
        dv = jnp.zeros(query.shape, F32)
        for which in range(2):
            mask = head_mask(query.shape, which)
            probs = head_probs(query, key, which, allowed)
            only = jnp.where(mask, do, zero)
            dp = dot(only, value, NT)
            ds = probs * (dp - jnp.sum(probs * dp, axis=-1, keepdims=True))
            ds = ds.astype(BF)
            dq = dq + dot(ds, jnp.where(mask, key, zero))
            dk = dk + dot(ds, jnp.where(mask, query, zero), TN)
            dv = dv + dot(probs.astype(BF), only, TN)
        dqkv[:, pl.ds(first, 2 * HD)] = (dq * 0.125).astype(BF)
        dqkv[:, pl.ds(width + first, 2 * HD)] = (dk * 0.125).astype(BF)
        dqkv[:, pl.ds(2 * width + first, 2 * HD)] = dv.astype(BF)
    part[...] = dot(dqkv[...], w_qkv[...], NT).astype(BF)


def last_body(mine, other, tokens, dr, norm, grad, sums):
    da1 = mine[...].astype(F32) + other[...].astype(F32)
    unit, scale = normalize(tokens[...].astype(F32))
    grad[...] = (dr[...] + normalize_back(da1, norm[0:1], unit, scale)).astype(BF)
    sums[0:1] = jnp.sum(da1 * unit, axis=0, keepdims=True)
    sums[1:2] = jnp.sum(da1, axis=0, keepdims=True)
    sums[2:8] = jnp.zeros((6, D), F32)


def call(body, name, shapes, *args):
    return pl.pallas_call(
        body,
        out_shape=[jax.ShapeDtypeStruct(s, d) for s, d in shapes],
        in_specs=[pl.BlockSpec(memory_space=pltpu.VMEM)] * len(args),
        out_specs=[pl.BlockSpec(memory_space=pltpu.VMEM)] * len(shapes),
        compiler_params=pltpu.CompilerParams(vmem_limit_bytes=VMEM_LIMIT),
        name=name,
    )(*args)


def pack_ext(norm, split):
    rows, columns = norm.shape[1], split.shape[1]

    def wide(values):
        return jnp.pad(values, ((0, 0), (0, 128 - values.shape[1])))

    hidden = split[2:6].T.reshape(1, 4 * columns)
    packed = jnp.concatenate([wide(hidden), wide(norm), wide(split[0:2])], axis=0)
    return jnp.pad(packed, ((0, EXT - packed.shape[0]), (0, 0)))


def local(count, *args):
    (tokens, cotangent, segments, w_qkv, w_out, w_fc, w_proj, vec_norm, vec_split) = args[:9]
    firsts, seconds = args[9:15], args[15:21]
    masters = (w_qkv, w_out, w_fc, w_proj, vec_norm, vec_split)
    rows = w_fc.shape[0]
    width = w_qkv.shape[2]
    hidden = w_fc.shape[1]
    piece = vec_split.shape[1]
    batches, length = tokens.shape[:2]
    total = batches * length
    blocks = (
        w_qkv.transpose(1, 0, 2).reshape(rows, 3 * width).astype(BF),
        w_out.T.astype(BF),
        w_fc.astype(BF),
        w_proj.T.astype(BF),
        pack_ext(vec_norm, vec_split).astype(BF),
    )
    got = gather(blocks, count)
    m_qkv, m_out, m_fc, m_proj = (got[i].reshape(D, got[i].shape[2]) for i in range(4))
    vectors = got[4].astype(F32)
    bias = vectors[:, 0, : 4 * piece].reshape(1, hidden)
    norm = vectors[:, 1:7, :rows].transpose(1, 0, 2).reshape(6, D)
    split = vectors[:, 7:9, :piece].transpose(1, 0, 2).reshape(2, width)
    norm = jnp.pad(norm, ((0, 2), (0, 0)))
    split = jnp.pad(split, ((0, 6), (0, 0)))

    t = tokens.reshape(total, D)
    cot = cotangent.reshape(total, D)
    seg = segments.reshape(total)
    place = jnp.arange(total)
    block = place // length
    allow = (
        (seg[:, None] == seg[None, :])
        & (block[:, None] == block[None, :])
        & (place[None, :] <= place[:, None])
    ).astype(F32)

    def swap(values):
        return lax.ppermute(values, "mp", [(0, 1), (1, 0)])

    a1, qkv, o, part = call(
        attend_body,
        "attend",
        [((total, D), BF), ((total, 3 * width), BF), ((total, width), BF), ((total, D), BF)],
        *(t, allow, norm, split, m_qkv, m_out),
    )
    r, a2, gl, dz, part2 = call(
        feed_body,
        "feed",
        [
            ((total, D), F32),
            ((total, D), BF),
            ((total, hidden), BF),
            ((total, hidden), BF),
            ((total, 2 * D), BF),
        ],
        *(t, part, swap(part), cot, norm, bias, m_fc, m_proj),
    )
    out, dr, dao, dqkv, part3, sums2 = call(
        back_body,
        "back",
        [
            ((total, D), BF),
            ((total, D), F32),
            ((total, D), BF),
            ((total, 3 * width), BF),
            ((total, D), BF),
            ((8, D), F32),
        ],
        *(part2, swap(part2), r, cot, allow, norm, qkv, m_out, m_qkv),
    )
    in_grad, sums1 = call(
        last_body,
        "last",
        [((total, D), BF), ((8, D), F32)],
        *(part3, swap(part3), t, dr, norm),
    )
    norm_sums = jnp.concatenate([sums1[0:2], sums2[0:4]], axis=0)
    stack_sums = jnp.sum(dqkv.astype(F32), axis=0)
    hidden_sums = jnp.sum(dz.astype(F32), axis=0)

    def wide(values):
        return jnp.pad(values, ((0, 0), (0, 0), (0, 128 - values.shape[2])))

    split_sums = jnp.stack([stack_sums[:width], stack_sums[2 * width :]])
    ext = jnp.concatenate(
        [
            wide(hidden_sums.reshape(count, 1, 4 * piece)),
            wide(norm_sums.reshape(6, count, rows).transpose(1, 0, 2)),
            wide(split_sums.reshape(2, count, piece).transpose(1, 0, 2)),
        ],
        axis=1,
    )
    ext = jnp.pad(ext, ((0, 0), (0, EXT - ext.shape[1]), (0, 0)))
    lhs = [v.T.reshape(count, rows, total) for v in (a1, dao, a2, cot)]
    g_qkv, g_out, g_fc, g_proj, g_ext = reduce_scatter(lhs, (dqkv, o, dz, gl), ext)
    reduced = (
        g_qkv.reshape(rows, 3, width).transpose(1, 0, 2),
        g_out.T,
        g_fc,
        g_proj.T,
        g_ext[1:7, :rows],
        jnp.concatenate([g_ext[7:9, :piece], g_ext[0, : 4 * piece].reshape(piece, 4).T]),
    )
    rates = rate_list()
    decays = (0.1, 0.1, 0.1, 0.1, 0.0, 0.0)
    updated = [
        adamw(masters[i], reduced[i], firsts[i], seconds[i], rates[i], decays[i])
        for i in range(6)
    ]
    return (
        out.reshape(tokens.shape),
        in_grad.reshape(tokens.shape),
        *(u[0] for u in updated),
        *(u[1] for u in updated),
        *(u[2] for u in updated),
    )


def solution(mesh):
    shards = (
        P(None, "dp", "mp"),
        P("mp", "dp"),
        P("dp", "mp"),
        P("mp", "dp"),
        P(None, "dp"),
        P(None, ("mp", "dp")),
    )
    rows = P(None, "dp", None)
    return jax.shard_map(
        functools.partial(local, mesh.shape["dp"]),
        mesh=mesh,
        in_specs=(rows, rows, P(None, "dp")) + shards * 3,
        out_specs=(rows, rows) + shards * 3,
        check_vma=False,
    )
```

time: 963 us -> 232 us (0.24)
  waiting for transfers between devices: 739 us -> 15.8 us
  Pallas kernels: 0 us -> 171 us
  matrix products: 71.4 us -> 0 us
  blocking collectives: 41.1 us -> 0 us
  local copies, waits for them, and re-layouts: 45.1 us -> 17.6 us
  other arithmetic: 47.6 us -> 20.4 us
  between operations: 15.8 us -> 0.93 us
    reduce_scatter x3 -> x0, waiting for transfers between devices: 271 us -> none  [the longest x1 105 us: local(): lax.psum_scatter(term_fc, 'dp', scatter_dimension=0, tiled=True)]
    unnamed x17 -> x0, waiting for transfers between devices: 253 us -> none
    pallas_call x0 -> x6, Pallas kernels: none -> 171 us  [the longest x1 73.2 us: reduce_scatter(): pl.pallas_call(functools.partial(reduce_kernel, chips, parts), out_shape=...]
    all_gather x4 -> x0, waiting for transfers between devices: 134 us -> none  [the longest x1 49.9 us: local(): lax.all_gather(send_fc, 'dp', axis=0, tiled=True)]
    psum x4 -> x0, waiting for transfers between devices: 81.6 us -> none  [the longest x2 40.4 us: local(): lax.psum(attn_part.astype(jnp.bfloat16), 'mp').astype(jnp.float32)]
    dot_general x36 -> x0, matrix products: 71.4 us -> none  [the longest x2 7.64 us: local(): jnp.dot(grad_mlp, back_proj.T, preferred_element_type=jnp.float32)]
    all_gather x2 -> x0, blocking collectives: 41.1 us -> none  [the longest x1 23.3 us: local(): lax.all_gather(send_split, 'dp', axis=1, tiled=True)]
    ppermute x0 -> x3, waiting for transfers between devices: none -> 15.8 us  [swap(): return lax.ppermute(values, 'mp', [(0, 1), (1, 0)])]
  transfers between devices with their start and end apart: 14 -> 3, of which waited for: 14 -> 3; matrix products, arithmetic and copies ran while one was open for 7% -> 4% of each run, Pallas kernels for 0% -> 0%
where the time goes in v1:
time: 232 us; the launch traced here: 231 us
  Pallas kernels  171 us (74%)
  other arithmetic  20.4 us (9%)
  local copies, waits for them, and re-layouts  17.6 us (8%)
  waiting for transfers between devices  15.8 us (7%)
  starting transfers between devices  4.62 us (2%)
    pallas_call x1, Pallas kernels, reduce_scatter(): pl.pallas_call(functools.partial(reduce_kernel, chips, parts), out_shape=...  73.2 us
    pallas_call x1, Pallas kernels, gather(): pl.pallas_call(functools.partial(gather_kernel, chips, parts), out_shape=...  73.2 us
    pallas_call x4, Pallas kernels, call(): pl.pallas_call(body, out_shape=[jax.ShapeDtypeStruct(s, d) for s, d in sh...  25 us
    ppermute x3, waiting for transfers between devices, swap(): return lax.ppermute(values, 'mp', [(0, 1), (1, 0)])  15.8 us
    sub x6, other arithmetic, adamw(): weight - step_rate * (scaled_first / (jnp.sqrt(scaled_second) + 1e-08) +...  9.03 us
    transpose x4, local copies, waits for them, and re-layouts, local(): lhs = [v.T.reshape(count, rows, total) for v in (a1, dao, a2, cot)]  5.27 us
  transfers between devices with their start and end apart: 3, of which 3 were waited for; matrix products, arithmetic and copies ran while one was open for 4% of the time, Pallas kernels for 0%

profile of v1, /device:TPU:0, one launch (start us, length us, event | category | flops | bytes accessed | tf_op | source)
XLA Modules:
  0.0 230.7 jit_solution(15965383077414308756)
XLA Ops:
  0.7 0.7 convert.17
  1.5 0.1 reshape.143
  1.6 0.7 convert.18
  2.3 1.0 convert_bitcast_fusion.1
  3.3 0.7 copy.111
  4.0 1.8 convert_bitcast_fusion.refs_3_
  5.8 1.8 convert_element_type.55.refs_2_
  7.5 1.5 convert_bitcast_fusion.2.refs_1_
  9.1 0.6 pad.37.refs_4_
  9.7 73.2 %gather_weights.1 = (bf16[16,64,1536]{2,1,0:T(8,128)(2,1)}, bf16[16,64,512]{2,1,0:T(8,128)(2,1)}, bf16[16,64,2048]{2,1,0:T(8,128)(2,1)}, bf16[16,64,2048]{2,1,0:T(8,128)(2,1)}, bf16[16,16,128]{2,1,0:T(8,128)(2,1)}) custom-call(bf16[64,1536]{1,0:T(8,128)(2,1)} %bitcast.91, bf16[64,512]{1,0:T(8,128)(2,1)} %convert_bitcast_fusion.2.refs_1_, ...), custom_call_target="tpu_custom_call" | custom-call | tf_op jit(solution)/shard_map/gather_weights/pallas_call | solution.py:169
  82.9 0.9 convert_element_type.58
  84.0 0.6 pad.38.norm
  84.6 0.6 pad.39.split
  85.3 0.7 fusion.10.allow
  86.0 5.6 %attend.1 = (bf16[128,1024]{1,0:T(8,128)(2,1)}, bf16[128,1536]{1,0:T(8,128)(2,1)}, bf16[128,512]{1,0:T(8,128)(2,1)}, bf16[128,1024]{1,0:T(8,128)(2,1)}) custom-call(bf16[128,1024]{1,0:T(8,128)(2,1)} %bitcast.84, f32[128,128]{1,0:T(8,128)} %fusion.10.allow, f32[8,1024]{1,0:T(8,128)} %pad.38.norm, f32[8,512]{1,0:T(8,128)} %pad.39.split, ...), custom_call_target="tpu_custom_call" | custom-call | tf_op jit(solution)/shard_map/attend/pallas_call | solution.py:458
  91.6 1.5 collective-permute-start
  93.2 0.6 slice_bitcast_fusion.2.bias
  93.8 6.6 %collective-permute-done.other = bf16[128,1024]{1,0:T(8,128)(2,1)S(1)} collective-permute-done((bf16[128,1024]{1,0:T(8,128)(2,1)}, bf16[128,1024]{1,0:T(8,128)(2,1)S(1)}, u32[]{:S(2)}, u32[]{:S(2)}) %collective-permute-start) | collective-permute-done | bytes 262176 | tf_op jit(solution)/shard_map/ppermute | solution.py:517
  100.4 0.7 copy-done.13
  101.1 9.4 %feed.1 = (f32[128,1024]{1,0:T(8,128)}, bf16[128,1024]{1,0:T(8,128)(2,1)}, bf16[128,2048]{1,0:T(8,128)(2,1)}, bf16[128,2048]{1,0:T(8,128)(2,1)}, bf16[128,2048]{1,0:T(8,128)(2,1)}) custom-call(bf16[128,1024]{1,0:T(8,128)(2,1)} %bitcast.85, bf16[128,1024]{1,0:T(8,128)(2,1)} %get-tuple-element.50.mine, bf16[128,1024]{1,0:T(8,128)(2,1)} %copy-done.13, ...), custom_call_target="tpu_custom_call" | custom-call | tf_op jit(solution)/shard_map/feed/pallas_call | solution.py:458
  110.5 1.5 collective-permute-start.1
  112.1 0.9 copy.103
  112.9 0.8 copy.106
  113.7 1.8 copy.105
  115.5 1.1 convert_reduce_fusion
  116.7 7.5 %collective-permute-done.1.other = bf16[128,2048]{1,0:T(8,128)(2,1)S(1)} collective-permute-done((bf16[128,2048]{1,0:T(8,128)(2,1)}, bf16[128,2048]{1,0:T(8,128)(2,1)S(1)}, u32[]{:S(2)}, u32[]{:S(2)}) %collective-permute-start.1) | collective-permute-done | bytes 524320 | tf_op jit(solution)/shard_map/ppermute | solution.py:517
  124.1 0.8 copy-done.8
  124.9 7.4 %back.1 = (bf16[128,1024]{1,0:T(8,128)(2,1)}, f32[128,1024]{1,0:T(8,128)}, bf16[128,1024]{1,0:T(8,128)(2,1)}, bf16[128,1536]{1,0:T(8,128)(2,1)}, bf16[128,1024]{1,0:T(8,128)(2,1)}, /*index=5*/f32[8,1024]{1,0:T(8,128)}) custom-call(bf16[128,2048]{1,0:T(8,128)(2,1)} %get-tuple-element.53.mine, bf16[128,2048]{1,0:T(8,128)(2,1)} %copy-done.8, ...), custom_call_target="tpu_custom_call" | custom-call | tf_op jit(solution)/shard_map/back/pallas_call | solution.py:458
  132.3 1.6 collective-permute-start.2
  133.9 0.8 slice.56
  134.7 1.1 convert_reduce_fusion.1
  135.9 1.8 copy.104
  137.7 1.7 collective-permute-done.2.other
  139.4 0.7 copy-done.15
  140.2 2.6 %last.1 = (bf16[128,1024]{1,0:T(8,128)(2,1)}, f32[8,1024]{1,0:T(8,128)}) custom-call(bf16[128,1024]{1,0:T(8,128)(2,1)} %get-tuple-element.57.mine, bf16[128,1024]{1,0:T(8,128)(2,1)} %copy-done.15, bf16[128,1024]{1,0:T(8,128)(2,1)} %bitcast.86, f32[128,1024]{1,0:T(8,128)} %get-tuple-element.58.dr, f32[8,1024]{1,0:T(8,128)} %pad.38.norm), custom_call_target="tpu_custom_call" | custom-call | tf_op jit(solution)/shard_map/last/pallas_call | solution.py:458
  142.7 0.8 slice.55
  143.7 0.7 pad.42.refs_8_
  144.3 73.2 %reduce_gradients.1 = (f32[64,1536]{1,0:T(8,128)}, f32[64,512]{1,0:T(8,128)}, f32[64,2048]{1,0:T(8,128)}, f32[64,2048]{1,0:T(8,128)}, f32[16,128]{1,0:T(8,128)}) custom-call(bf16[16,64,128]{2,1,0:T(8,128)(2,1)} %bitcast.87, bf16[16,64,128]{2,1,0:T(8,128)(2,1)} %bitcast.90, bf16[16,64,128]{2,1,0:T(8,128)(2,1)} %bitcast.89, bf16[16,64,128]{2,1,0:T(8,128)(2,1)} %bitcast.88, ...), custom_call_target="tpu_custom_call" | custom-call | tf_op jit(solution)/shard_map/reduce_gradients/pallas_call | solution.py:312
  217.5 1.3 slice_reduce_fusion
  218.8 1.3 slice.60
  220.0 0.7 reshape_squeeze.7
  220.8 0.7 copy.109
  221.5 1.4 multiply_subtract_fusion.5
  222.9 2.5 %multiply_subtract_fusion = (f32[2048,64]{0,1:T(8,128)}, f32[2048,64]{0,1:T(8,128)}, f32[2048,64]{0,1:T(8,128)}) fusion(f32[2048,64]{0,1:T(8,128)S(1)} %copy-done.1, f32[64,2048]{1,0:T(8,128)} %get-tuple-element.72, f32[2048,64]{0,1:T(8,128)S(1)} %copy-done.4, f32[2048,64]{0,1:T(8,128)S(1)} %copy-done.5), kind=kLoop, calls=%fused_computation.9 | loop fusion | flops 1966080 | bytes 3670016 | tf_op jit(solution)/shard_map/sub | solution.py:47
  225.5 2.4 %multiply_subtract_fusion.1 = (f32[64,2048]{1,0:T(8,128)}, f32[64,2048]{1,0:T(8,128)}, f32[64,2048]{1,0:T(8,128)}) fusion(f32[64,2048]{1,0:T(8,128)S(1)} %copy-done.2, f32[64,2048]{1,0:T(8,128)} %get-tuple-element.71, f32[64,2048]{1,0:T(8,128)S(1)} %copy-done.6, f32[64,2048]{1,0:T(8,128)S(1)} %copy-done.7), kind=kLoop, calls=%fused_computation.10 | loop fusion | flops 1966080 | bytes 3670016 | tf_op jit(solution)/shard_map/sub | solution.py:47
  228.0 1.2 multiply_subtract_fusion.2
  229.2 0.8 multiply_subtract_fusion.3
  230.0 0.6 multiply_subtract_fusion.4
  (67 shorter events, 0.9 us)
Async XLA Ops:
  0.7 84.5 %copy-start.24 = (s32[2,64]{1,0:T(2,128)S(1)}, s32[2,64]{1,0:T(2,128)}, u32[]{:S(2)}) copy-start(s32[2,64]{1,0:T(2,128)} %param.23) | copy-start | bytes 1540
  91.6 8.8 %collective-permute-start = (bf16[128,1024]{1,0:T(8,128)(2,1)}, bf16[128,1024]{1,0:T(8,128)(2,1)S(1)}, u32[]{:S(2)}, u32[]{:S(2)}) collective-permute-start(bf16[128,1024]{1,0:T(8,128)(2,1)} %get-tuple-element.50.mine), channel_id=1, source_target_pairs={{0,1},{1,0},{2,3},{3,2},{4,5},{5,4},{6,7},{7,6},{8,9},{9,8},{10,11... | collective-permute-start | bytes 786440 | tf_op jit(solution)/shard_map/ppermute | solution.py:517
  100.4 0.7 copy-start.13
  101.1 10.9 %copy-start.14 = (bf16[128,1024]{1,0:T(8,128)(2,1)S(1)}, bf16[128,1024]{1,0:T(8,128)(2,1)}, u32[]{:S(2)}) copy-start(bf16[128,1024]{1,0:T(8,128)(2,1)} %get-tuple-element.60) | copy-start | bytes 786436
  101.1 11.8 %copy-start = (bf16[2,64,1024]{2,1,0:T(8,128)(2,1)S(1)}, bf16[2,64,1024]{2,1,0:T(8,128)(2,1)}, u32[]{:S(2)}) copy-start(bf16[2,64,1024]{2,1,0:T(8,128)(2,1)} %param.22) | copy-start | bytes 786436
  110.5 13.6 %collective-permute-start.1 = (bf16[128,2048]{1,0:T(8,128)(2,1)}, bf16[128,2048]{1,0:T(8,128)(2,1)S(1)}, u32[]{:S(2)}, u32[]{:S(2)}) collective-permute-start(bf16[128,2048]{1,0:T(8,128)(2,1)} %get-tuple-element.53.mine), channel_id=1, source_target_pairs={{0,1},{1,0},{2,3},{3,2},{4,5},{5,4},{6,7},{7,6},{8,9},{9,8},{10,11... | collective-permute-start | bytes 1572872 | tf_op jit(solution)/shard_map/ppermute | solution.py:517
  124.1 0.8 copy-start.8
  132.3 90.6 %copy-start.1 = (f32[2048,64]{0,1:T(8,128)S(1)}, f32[2048,64]{0,1:T(8,128)}, u32[]{:S(2)}) copy-start(f32[2048,64]{0,1:T(8,128)} %param.27) | copy-start | bytes 1572868
  132.3 90.6 %copy-start.4 = (f32[2048,64]{0,1:T(8,128)S(1)}, f32[2048,64]{0,1:T(8,128)}, u32[]{:S(2)}) copy-start(f32[2048,64]{0,1:T(8,128)} %param.33) | copy-start | bytes 1572868
  132.3 90.6 %copy-start.5 = (f32[2048,64]{0,1:T(8,128)S(1)}, f32[2048,64]{0,1:T(8,128)}, u32[]{:S(2)}) copy-start(f32[2048,64]{0,1:T(8,128)} %param.39) | copy-start | bytes 1572868
  132.3 7.1 %collective-permute-start.2 = (bf16[128,1024]{1,0:T(8,128)(2,1)}, bf16[128,1024]{1,0:T(8,128)(2,1)S(1)}, u32[]{:S(2)}, u32[]{:S(2)}) collective-permute-start(bf16[128,1024]{1,0:T(8,128)(2,1)} %get-tuple-element.57.mine), channel_id=1, source_target_pairs={{0,1},{1,0},{2,3},{3,2},{4,5},{5,4},{6,7},{7,6},{8,9},{9,8},{10,11... | collective-permute-start | bytes 786440 | tf_op jit(solution)/shard_map/ppermute | solution.py:517
  139.4 0.7 copy-start.15
  140.1 85.3 %copy-start.2 = (f32[64,2048]{1,0:T(8,128)S(1)}, f32[64,2048]{1,0:T(8,128)}, u32[]{:S(2)}) copy-start(f32[64,2048]{1,0:T(8,128)} %param.26) | copy-start | bytes 1572868
  140.1 85.3 %copy-start.6 = (f32[64,2048]{1,0:T(8,128)S(1)}, f32[64,2048]{1,0:T(8,128)}, u32[]{:S(2)}) copy-start(f32[64,2048]{1,0:T(8,128)} %param.32) | copy-start | bytes 1572868
  140.1 85.3 %copy-start.7 = (f32[64,2048]{1,0:T(8,128)S(1)}, f32[64,2048]{1,0:T(8,128)}, u32[]{:S(2)}) copy-start(f32[64,2048]{1,0:T(8,128)} %param.38) | copy-start | bytes 1572868
  217.5 10.4 %copy-start.3 = (f32[3,64,512]{2,1,0:T(8,128)S(1)}, f32[3,64,512]{2,1,0:T(8,128)}, u32[]{:S(2)}) copy-start(f32[3,64,512]{2,1,0:T(8,128)} %param.24) | copy-start | bytes 1179652
  221.4 6.5 %copy-start.10 = (f32[3,64,512]{2,1,0:T(8,128)S(1)}, f32[3,64,512]{2,1,0:T(8,128)}, u32[]{:S(2)}) copy-start(f32[3,64,512]{2,1,0:T(8,128)} %param.30) | copy-start | bytes 1179652
  221.5 6.5 %copy-start.11 = (f32[3,64,512]{2,1,0:T(8,128)S(1)}, f32[3,64,512]{2,1,0:T(8,128)}, u32[]{:S(2)}) copy-start(f32[3,64,512]{2,1,0:T(8,128)} %param.36) | copy-start | bytes 1179652
  221.5 6.5 %copy-start.12 = (f32[64,1536]{1,0:T(8,128)S(1)}, f32[64,1536]{1,0:T(8,128)}, u32[]{:S(2)}) copy-start(f32[64,1536]{1,0:T(8,128)} %get-tuple-element.69) | copy-start | bytes 1179652
  222.9 6.3 %copy-start.9 = (f32[512,64]{0,1:T(8,128)S(1)}, f32[512,64]{0,1:T(8,128)}, u32[]{:S(2)}) copy-start(f32[512,64]{0,1:T(8,128)} %param.25) | copy-start | bytes 393220
  222.9 6.3 %copy-start.16 = (f32[512,64]{0,1:T(8,128)S(1)}, f32[512,64]{0,1:T(8,128)}, u32[]{:S(2)}) copy-start(f32[512,64]{0,1:T(8,128)} %param.31) | copy-start | bytes 393220
  222.9 6.3 %copy-start.17 = (f32[512,64]{0,1:T(8,128)S(1)}, f32[512,64]{0,1:T(8,128)}, u32[]{:S(2)}) copy-start(f32[512,64]{0,1:T(8,128)} %param.37) | copy-start | bytes 393220
  222.9 6.3 %copy-start.18 = (f32[64,512]{1,0:T(8,128)S(1)}, f32[64,512]{1,0:T(8,128)}, u32[]{:S(2)}) copy-start(f32[64,512]{1,0:T(8,128)} %get-tuple-element.70) | copy-start | bytes 393220
  225.4 4.6 %copy-start.19 = (f32[6,32]{1,0:T(8,128)S(1)}, f32[6,32]{1,0:T(8,128)}, u32[]{:S(2)}) copy-start(f32[6,32]{1,0:T(8,128)} %param.29) | copy-start | bytes 2308
  225.4 4.6 %copy-start.20 = (f32[4,32]{1,0:T(4,128)S(1)}, f32[4,32]{1,0:T(4,128)}, u32[]{:S(2)}) copy-start(f32[4,32]{1,0:T(4,128)} %copy.109) | copy-start | bytes 1540
  225.4 4.6 %copy-start.21 = (f32[2,32]{1,0:T(2,128)S(1)}, f32[2,32]{1,0:T(2,128)}, u32[]{:S(2)}) copy-start(f32[2,32]{1,0:T(2,128)} %slice.60) | copy-start | bytes 772
  225.5 4.6 %copy-start.22 = (f32[6,32]{1,0:T(8,128)S(1)}, f32[6,32]{1,0:T(8,128)}, u32[]{:S(2)}) copy-start(f32[6,32]{1,0:T(8,128)} %param.35) | copy-start | bytes 2308
  225.5 4.6 %copy-start.23 = (f32[6,32]{1,0:T(8,128)S(1)}, f32[6,32]{1,0:T(8,128)}, u32[]{:S(2)}) copy-start(f32[6,32]{1,0:T(8,128)} %param.41) | copy-start | bytes 2308

commit v2 on v1

--- a/solution.py
+++ b/solution.py
@@ -476,16 +476,435 @@
     return jnp.pad(packed, ((0, EXT - packed.shape[0]), (0, 0)))
 
 
-def local(count, *args):
-    (tokens, cotangent, segments, w_qkv, w_out, w_fc, w_proj, vec_norm, vec_split) = args[:9]
-    firsts, seconds = args[9:15], args[15:21]
-    masters = (w_qkv, w_out, w_fc, w_proj, vec_norm, vec_split)
-    rows = w_fc.shape[0]
+def mega_kernel(chips, *refs):
+    (tokens, cot, allow, i_qkv, i_out, i_fc, i_proj, i_ext) = refs[:8]
+    out, grad = refs[8:10]
+    outs = refs[10:15]
+    full = refs[15:20]
+    bufs = refs[20:25]
+    terms = refs[25:30]
+    left, right = refs[30:34], refs[34:38]
+    (norm, split, bias, qkv, r, a2, slope, dr, ext, ext_other) = refs[38:48]
+    mine, other = refs[48:51], refs[51:54]
+    (g_send, g_recv, gs_send, gs_recv, r_send, r_recv, s_send, s_recv, m_send, m_recv) = refs[54:]
+
+    count = 2 * chips
+    rows = i_fc.shape[0]
+    total = tokens.shape[0]
+    width = i_out.shape[0]
+    hidden = i_fc.shape[1]
+    me, sibling, place, device = ring_place(chips)
+    peer = 1 - lax.axis_index("mp")
+    neighbours = (device(place + 1), device(place - 1))
+    greet(
+        [{"dp": neighbours[0]}, {"dp": neighbours[1]}, {"dp": sibling}, {"mp": peer}]
+    )
+
+    h_qkv, h_out, q_ff = 3 * width // 2, width // 2, hidden // 4
+    groups = (
+        [(4, 0, 128, 0), (0, 0, h_qkv, 0), (0, h_qkv, h_qkv, 1)]
+        + [(1, 0, h_out, 0), (1, h_out, h_out, 1)],
+        [(2, j * q_ff, q_ff, j % 2) for j in range(4)],
+        [(3, j * q_ff, q_ff, j % 2) for j in range(4)],
+    )
+    parts, members = [], []
+    for group in groups:
+        members.append(list(range(len(parts), len(parts) + len(group))))
+        parts += group
+
+    def rows_of(index, owner):
+        high = EXT if index == 4 else rows
+        return pl.ds(pl.multiple_of(owner * high, high), high)
+
+    def block(k, step):
+        index, first, wide, way = parts[k]
+        owner = device(place - step if way == 0 else place + step)
+        return full[index].at[rows_of(index, owner), pl.ds(first, wide)]
+
+    def ring_copy(k, step):
+        ref = block(k, step)
+        return remote(ref, ref, g_send.at[k, step], g_recv.at[k, step], neighbours[parts[k][3]])
+
+    def side_copy(k, step):
+        ref = block(k, step)
+        return remote(ref, ref, gs_send.at[k, step], gs_recv.at[k, step], sibling)
+
+    def gather_step(group, step):
+        for k in members[group]:
+            if step > 0:
+                ring_copy(k, step - 1).wait_recv()
+            if step < chips - 1:
+                ring_copy(k, step).start()
+            side_copy(k, step).start()
+
+    def gather_end(group):
+        for k in members[group]:
+            for step in range(chips):
+                side_copy(k, step).wait_recv()
+
+    def to_side(m):
+        pairs = (
+            (left[m].at[:, pl.ds(0, total)], left[m].at[:, pl.ds(total, total)]),
+            (right[m].at[pl.ds(0, total)], right[m].at[pl.ds(total, total)]),
+        )
+        return [
+            remote(src, dst, s_send.at[2 * m + j], s_recv.at[2 * m + j], sibling)
+            for j, (src, dst) in enumerate(pairs)
+        ]
+
+    side_ext = remote(ext, ext_other, s_send.at[8], s_recv.at[8], sibling)
+
+    def to_peer(j):
+        return pltpu.make_async_remote_copy(
+            src_ref=mine[j],
+            dst_ref=other[j],
+            send_sem=m_send.at[j],
+            recv_sem=m_recv.at[j],
+            device_id={"mp": peer},
+            device_id_type=pl.DeviceIdType.MESH,
+        )
+
+    def flip(values):
+        return values.astype(F32).T.astype(BF)
+
+    def reduce_rows(index, k, step):
+        way = parts[k][3]
+        owner = device(place - 1 - step if way == 0 else place + 1 + step)
+        return rows_of(index, owner)
+
+    def term(k, step):
+        index, first, wide, _ = parts[k]
+        at = reduce_rows(index, k, step)
+        if index == 4:
+            return ext[at, :] + ext_other[at, :]
+        return dot(left[index][at, :], right[index][:, pl.ds(first, wide)])
+
+    def sum_copy(k, step):
+        index, first, wide, way = parts[k]
+        columns = pl.ds(first, wide)
+        return remote(
+            bufs[index].at[step, :, columns],
+            bufs[index].at[step + 1, :, columns],
+            r_send.at[k, step],
+            r_recv.at[k, step],
+            neighbours[way],
+        )
+
+    def reduce_step(ks, step):
+        if step == 0:
+            for k in ks:
+                index, first, wide, _ = parts[k]
+                bufs[index][0, :, pl.ds(first, wide)] = term(k, 0).astype(BF)
+                sum_copy(k, 0).start()
+            return
+        for k in ks:
+            index, first, wide, _ = parts[k]
+            terms[index][:, pl.ds(first, wide)] = term(k, step)
+        for k in ks:
+            index, first, wide, _ = parts[k]
+            columns = pl.ds(first, wide)
+            sum_copy(k, step - 1).wait_recv()
+            value = bufs[index][step, :, columns].astype(F32) + terms[index][:, columns]
+            if step < chips - 1:
+                bufs[index][step, :, columns] = value.astype(BF)
+                sum_copy(k, step).start()
+            else:
+                outs[index][:, columns] = value
+
+    own = rows_of(0, me)
+    full[4][rows_of(4, me), :] = i_ext[...].astype(BF)
+    for t in range(3):
+        full[0][own, pl.ds(t * width, width)] = i_qkv[t].astype(BF)
+    full[1][own, :] = i_out[...].T.astype(BF)
+    gather_step(0, 0)
+    full[2][own, :] = i_fc[...].astype(BF)
+    full[3][own, :] = i_proj[...].T.astype(BF)
+    left[3][:, pl.ds(0, total)] = flip(cot[...])
+    here = pl.ds(0, total)
+
+    def vectors():
+        for j in range(count):
+            bias[:, pl.ds(j * 128, 128)] = full[4][pl.ds(j * EXT, EXT), :].astype(F32)
+        each = 128 // rows
+        for j in range(count // each):
+            norm[:, pl.ds(j * 128, 128)] = sum(
+                full[4][pl.ds((j * each + i) * EXT, EXT), :].astype(F32) for i in range(each)
+            )
+        each = count * 128 // width
+        for j in range(count // each):
+            split[:, pl.ds(j * 128, 128)] = sum(
+                full[4][pl.ds((j * each + i) * EXT, EXT), :].astype(F32) for i in range(each)
+            )
+
+    def first_norm():
+        vectors()
+        unit, _ = normalize(tokens[...].astype(F32))
+        mine[0][...] = (unit * norm[1:2] + norm[2:3]).astype(BF)
+        left[0][:, here] = flip(mine[0][...])
+
+    def project(t):
+        columns = pl.ds(t * width, width)
+        values = dot(mine[0][...], full[0][:, columns])
+        if t != 1:
+            values = values + split[pl.ds(7 + t // 2, 1)]
+        qkv[:, columns] = values.astype(BF)
+
+    def heads_of(pair):
+        first = pair * 2 * HD
+        return [qkv[:, pl.ds(t * width + first, 2 * HD)] for t in range(3)]
+
+    def attend(pair):
+        query, key, value = heads_of(pair)
+        allowed = allow[...] > 0.5
+        result = jnp.zeros(query.shape, F32)
+        for which in range(2):
+            probs = head_probs(query, key, which, allowed).astype(BF)
+            only = jnp.where(head_mask(value.shape, which), value, jnp.zeros_like(value))
+            result = result + dot(probs, only)
+        right[1][here, pl.ds(pair * 2 * HD, 2 * HD)] = result.astype(BF)
+
+    def attend_out():
+        mine[0][...] = dot(right[1][here, :], full[1][...], NT).astype(BF)
+        to_peer(0).start()
+
+    def second_norm():
+        to_peer(0).wait()
+        values = tokens[...].astype(F32) + (mine[0][...].astype(F32) + other[0][...].astype(F32))
+        values = values + norm[5:6]
+        r[...] = values
+        unit, _ = normalize(values)
+        a2[...] = (unit * norm[3:4] + norm[4:5]).astype(BF)
+        left[2][:, here] = flip(a2[...])
+
+    root = math.sqrt(2.0 / math.pi)
+
+    def gelu(j):
+        columns = pl.ds(j * q_ff, q_ff)
+        z = dot(a2[...], full[2][:, columns]) + bias[0:1, columns]
+        bent = jnp.tanh(root * (z + 0.044715 * z * z * z))
+        right[3][here, columns] = (0.5 * z * (1.0 + bent)).astype(BF)
+        slope[:, columns] = 0.5 * (1.0 + bent) + 0.5 * z * (1.0 - bent * bent) * root * (
+            1.0 + 3.0 * 0.044715 * z * z
+        )
+
+    def start_all(copies):
+        for copy in copies:
+            copy.start()
+
+    def wait_all(copies):
+        for copy in copies:
+            copy.wait()
+
+    pairs = width // (2 * HD)
+    lag = chips // 2
+    units = [
+        [lambda: gather_end(0), first_norm, lambda: project(0)],
+        [lambda: project(1), lambda: project(2)],
+        [lambda j=j: attend(j) for j in range(pairs)],
+        [attend_out],
+        [lambda: gather_end(1)],
+        [second_norm],
+        [lambda: gelu(0), lambda: gelu(1)],
+        [lambda: gelu(2), lambda: gelu(3), lambda: start_all(to_side(3))],
+    ]
+    for tick in range(2 * lag + chips):
+        for group in range(3):
+            step = tick - lag * group
+            if 0 <= step < chips and (group, step) != (0, 0):
+                gather_step(group, step)
+        if tick >= chips:
+            for unit in units[tick - chips]:
+                unit()
+    gather_end(2)
+
+    def gate_back(j):
+        columns = pl.ds(j * q_ff, q_ff)
+        right[2][here, columns] = (
+            slope[:, columns] * dot(cot[...], full[3][:, columns])
+        ).astype(BF)
+
+    def feed_out():
+        mine[1][:, pl.ds(0, D)] = dot(right[3][here, :], full[3][...], NT).astype(BF)
+
+    def feed_back():
+        mine[1][:, pl.ds(D, D)] = dot(right[2][here, :], full[2][...], NT).astype(BF)
+        to_peer(1).start()
+
+    def second_back():
+        to_peer(1).wait()
+        out[...] = (
+            r[...]
+            + (mine[1][:, pl.ds(0, D)].astype(F32) + other[1][:, pl.ds(0, D)].astype(F32))
+            + norm[6:7]
+        ).astype(BF)
+        da2 = mine[1][:, pl.ds(D, D)].astype(F32) + other[1][:, pl.ds(D, D)].astype(F32)
+        unit, scale = normalize(r[...])
+        top = cot[...].astype(F32)
+        value = top + normalize_back(da2, norm[3:4], unit, scale)
+        dr[...] = value
+        a2[...] = value.astype(BF)
+        left[1][:, here] = flip(a2[...])
+        sums = [da2 * unit, da2, value, top]
+        for j in range(4):
+            line = jnp.sum(sums[j], axis=0, keepdims=True)
+            for d in range(count):
+                ext[pl.ds(d * EXT + 3 + j, 1), :] = line[:, d * rows // 128 * 128 :][:, :128]
+
+    def heads_back():
+        r[:, pl.ds(0, width)] = dot(a2[...], full[1][...])
+
+    def attend_back(pair):
+        query, key, value = heads_of(pair)
+        first = pair * 2 * HD
+        do = r[:, pl.ds(first, 2 * HD)].astype(BF)
+        allowed = allow[...] > 0.5
+        zero = jnp.zeros_like(query)
+        dq = jnp.zeros(query.shape, F32)
+        dk = jnp.zeros(query.shape, F32)
+        dv = jnp.zeros(query.shape, F32)
+        for which in range(2):
+            mask = head_mask(query.shape, which)
+            probs = head_probs(query, key, which, allowed)
+            only = jnp.where(mask, do, zero)
+            dp = dot(only, value, NT)
+            ds = probs * (dp - jnp.sum(probs * dp, axis=-1, keepdims=True))
+            ds = ds.astype(BF)
+            dq = dq + dot(ds, jnp.where(mask, key, zero))
+            dk = dk + dot(ds, jnp.where(mask, query, zero), TN)
+            dv = dv + dot(probs.astype(BF), only, TN)
+        right[0][here, pl.ds(first, 2 * HD)] = (dq * 0.125).astype(BF)
+        right[0][here, pl.ds(width + first, 2 * HD)] = (dk * 0.125).astype(BF)
+        right[0][here, pl.ds(2 * width + first, 2 * HD)] = dv.astype(BF)
+
+    def attend_in():
+        mine[2][...] = dot(right[0][here, :], full[0][...], NT).astype(BF)
+        to_peer(2).start()
+
+    def first_back():
+        to_peer(2).wait()
+        da1 = mine[2][...].astype(F32) + other[2][...].astype(F32)
+        unit, scale = normalize(tokens[...].astype(F32))
+        grad[...] = (dr[...] + normalize_back(da1, norm[1:2], unit, scale)).astype(BF)
+        lines = [jnp.sum(da1 * unit, axis=0, keepdims=True), jnp.sum(da1, axis=0, keepdims=True)]
+        heads = jnp.sum(right[0][here, :].astype(F32), axis=0, keepdims=True)
+        gates = jnp.sum(right[2][here, :].astype(F32), axis=0, keepdims=True)
+        each = count * 128 // width
+        for d in range(count):
+            ext[pl.ds(d * EXT, 1), :] = gates[:, d * 128 : (d + 1) * 128]
+            for j in range(2):
+                ext[pl.ds(d * EXT + 1 + j, 1), :] = lines[j][:, d * rows // 128 * 128 :][:, :128]
+                at = 2 * j * width + d // each * 128
+                ext[pl.ds(d * EXT + 7 + j, 1), :] = heads[:, at : at + 128]
+        side_ext.start()
+
+    ext[...] = jnp.zeros(ext.shape, F32)
+    waves = (
+        (members[2], 0, lambda: wait_all(to_side(3))),
+        (members[1], 3, lambda: wait_all(to_side(2))),
+        (members[0][1:], 8, lambda: wait_all(to_side(0) + to_side(1))),
+        (members[0][:1], 9, side_ext.wait),
+    )
+    units = [
+        [lambda: gate_back(0), lambda: gate_back(1), lambda: gate_back(2)]
+        + [lambda: gate_back(3), lambda: start_all(to_side(2))],
+        [feed_back, feed_out],
+        [],
+        [],
+        [second_back, lambda: start_all(to_side(1))],
+        [heads_back] + [lambda j=j: attend_back(j) for j in range(pairs // 2)],
+        [lambda j=j: attend_back(j) for j in range(pairs // 2, pairs)]
+        + [lambda: start_all(to_side(0))],
+        [attend_in],
+        [first_back],
+    ]
+    units[1] = [feed_out, feed_back]
+    for tick in range(9 + chips):
+        for ks, begin, ready in waves:
+            step = tick - begin
+            if step == 0:
+                ready()
+            if 0 <= step < chips:
+                reduce_step(ks, step)
+        if tick < len(units):
+            for unit in units[tick]:
+                unit()
+
+    for k in range(len(parts)):
+        for step in range(chips - 1):
+            ring_copy(k, step).wait_send()
+            sum_copy(k, step).wait_send()
+        for step in range(chips):
+            side_copy(k, step).wait_send()
+
+
+def mega(count, tokens, cot, allow, w_qkv, w_out, w_fc, w_proj, ext):
+    chips = count // 2
+    total = tokens.shape[0]
+    rows, hidden = w_fc.shape
+    width = w_out.shape[0]
+    widths = (3 * width, width, hidden, hidden, 128)
+    heights = (rows, rows, rows, rows, EXT)
+    scratch = [pltpu.VMEM((count * h, w), BF) for h, w in zip(heights, widths)]
+    scratch += [pltpu.VMEM((chips, h, w), BF) for h, w in zip(heights, widths)]
+    scratch += [pltpu.VMEM((h, w), F32) for h, w in zip(heights, widths)]
+    scratch += [pltpu.VMEM((D, 2 * total), BF) for _ in range(4)]
+    scratch += [pltpu.VMEM((2 * total, w), BF) for w in widths[:4]]
+    scratch += [
+        pltpu.VMEM((EXT, D), F32),
+        pltpu.VMEM((EXT, width), F32),
+        pltpu.VMEM((EXT, hidden), F32),
+        pltpu.VMEM((total, 3 * width), BF),
+        pltpu.VMEM((total, D), F32),
+        pltpu.VMEM((total, D), BF),
+        pltpu.VMEM((total, hidden), F32),
+        pltpu.VMEM((total, D), F32),
+        pltpu.VMEM((count * EXT, 128), F32),
+        pltpu.VMEM((count * EXT, 128), F32),
+    ]
+    scratch += [pltpu.VMEM((total, w), BF) for w in (D, 2 * D, D)] * 2
+    n_parts = 13
+    sem = pltpu.SemaphoreType.DMA
+    scratch += [sem((n_parts, chips - 1))] * 2 + [sem((n_parts, chips))] * 2
+    scratch += [sem((n_parts, chips - 1))] * 2 + [sem((9,))] * 2 + [sem((3,))] * 2
+    shapes = [((total, D), BF)] * 2 + [((h, w), F32) for h, w in zip(heights, widths)]
+    return pl.pallas_call(
+        functools.partial(mega_kernel, chips),
+        out_shape=[jax.ShapeDtypeStruct(s, d) for s, d in shapes],
+        in_specs=[pl.BlockSpec(memory_space=pltpu.VMEM)] * 8,
+        out_specs=[pl.BlockSpec(memory_space=pltpu.VMEM)] * 7,
+        scratch_shapes=scratch,
+        compiler_params=pltpu.CompilerParams(
+            collective_id=2, has_side_effects=True, vmem_limit_bytes=VMEM_LIMIT
+        ),
+        name="train_step",
+    )(tokens, cot, allow, w_qkv, w_out, w_fc, w_proj, ext)
+
+
+def lanes_of(values, piece):
+    return lax.rem(lax.axis_index("dp"), 128 // piece)
+
+
+def pack_lanes(norm, split):
+    def put(values):
+        piece = values.shape[1]
+        spread = jnp.tile(values, (1, 128 // piece))
+        lane = jnp.arange(128) // piece
+        return jnp.where(lane == lanes_of(values, piece), spread, 0.0)
+
+    hidden = split[2:6].T.reshape(1, -1)
+    packed = jnp.concatenate([hidden, put(norm), put(split[0:2])], axis=0)
+    return jnp.pad(packed, ((0, EXT - packed.shape[0]), (0, 0)))
+
+
+def pick_lanes(values, piece):
+    return lax.dynamic_slice_in_dim(values, lanes_of(values, piece) * piece, piece, axis=1)
+
+
+def by_calls(count, t, cot, allow, w_qkv, w_out, w_fc, w_proj, vec_norm, vec_split):
+    rows, hidden = w_fc.shape
     width = w_qkv.shape[2]
-    hidden = w_fc.shape[1]
     piece = vec_split.shape[1]
-    batches, length = tokens.shape[:2]
-    total = batches * length
+    total = t.shape[0]
     blocks = (
         w_qkv.transpose(1, 0, 2).reshape(rows, 3 * width).astype(BF),
         w_out.T.astype(BF),
@@ -501,17 +920,6 @@
     split = vectors[:, 7:9, :piece].transpose(1, 0, 2).reshape(2, width)
     norm = jnp.pad(norm, ((0, 2), (0, 0)))
     split = jnp.pad(split, ((0, 6), (0, 0)))
-
-    t = tokens.reshape(total, D)
-    cot = cotangent.reshape(total, D)
-    seg = segments.reshape(total)
-    place = jnp.arange(total)
-    block = place // length
-    allow = (
-        (seg[:, None] == seg[None, :])
-        & (block[:, None] == block[None, :])
-        & (place[None, :] <= place[:, None])
-    ).astype(F32)
 
     def swap(values):
         return lax.ppermute(values, "mp", [(0, 1), (1, 0)])
@@ -580,6 +988,51 @@
         g_ext[1:7, :rows],
         jnp.concatenate([g_ext[7:9, :piece], g_ext[0, : 4 * piece].reshape(piece, 4).T]),
     )
+    return out, in_grad, reduced
+
+
+def by_one(count, t, cot, allow, w_qkv, w_out, w_fc, w_proj, vec_norm, vec_split):
+    rows = w_fc.shape[0]
+    width = w_qkv.shape[2]
+    piece = vec_split.shape[1]
+    ext = pack_lanes(vec_norm, vec_split)
+    out, in_grad, g_qkv, g_out, g_fc, g_proj, g_ext = mega(
+        count, t, cot, allow, w_qkv, w_out, w_fc, w_proj, ext
+    )
+    reduced = (
+        g_qkv.reshape(rows, 3, width).transpose(1, 0, 2),
+        g_out.T,
+        g_fc,
+        g_proj.T,
+        pick_lanes(g_ext[1:7], rows),
+        jnp.concatenate([pick_lanes(g_ext[7:9], piece), g_ext[0].reshape(piece, 4).T]),
+    )
+    return out, in_grad, reduced
+
+
+def local(count, *args):
+    (tokens, cotangent, segments, w_qkv, w_out, w_fc, w_proj, vec_norm, vec_split) = args[:9]
+    firsts, seconds = args[9:15], args[15:21]
+    masters = (w_qkv, w_out, w_fc, w_proj, vec_norm, vec_split)
+    rows = w_fc.shape[0]
+    piece = vec_split.shape[1]
+    batches, length = tokens.shape[:2]
+    total = batches * length
+    t = tokens.reshape(total, D)
+    cot = cotangent.reshape(total, D)
+    seg = segments.reshape(total)
+    place = jnp.arange(total)
+    block = place // length
+    allow = (
+        (seg[:, None] == seg[None, :])
+        & (block[:, None] == block[None, :])
+        & (place[None, :] <= place[:, None])
+    ).astype(F32)
+
+    form = by_one if rows == 64 and 4 * piece == 128 else by_calls
+    out, in_grad, reduced = form(
+        count, t, cot, allow, w_qkv, w_out, w_fc, w_proj, vec_norm, vec_split
+    )
     rates = rate_list()
     decays = (0.1, 0.1, 0.1, 0.1, 0.0, 0.0)
     updated = [

time: 232 us -> 183 us (0.79)
  waiting for transfers between devices: 15.8 us -> 0 us
  other arithmetic: 20.4 us -> 8.68 us
  Pallas kernels: 171 us -> 162 us
  local copies, waits for them, and re-layouts: 17.6 us -> 11.1 us
  starting transfers between devices: 4.62 us -> 0 us
    ppermute x3 -> x0, waiting for transfers between devices: 15.8 us -> none  [swap(): return lax.ppermute(values, 'mp', [(0, 1), (1, 0)])]
    pallas_call x6 -> x1, Pallas kernels: 171 us -> 162 us  [mega(): pl.pallas_call(functools.partial(mega_kernel, chips), out_shape=[jax.Shap...]
    unnamed x50 -> x54, local copies, waits for them, and re-layouts: 2.29 us -> 8.94 us
    convert_element_type x4 -> x0, other arithmetic: 5.93 us -> none  [the longest x1 1.77 us: local(): w_proj.T.astype(BF)]
    transpose x11 -> x3, local copies, waits for them, and re-layouts: 6.07 us -> 0.17 us  [the longest x2 0.09 us: pack_lanes(): hidden = split[2:6].T.reshape(1, -1)]
    ppermute x3 -> x0, starting transfers between devices: 4.62 us -> none  [swap(): return lax.ppermute(values, 'mp', [(0, 1), (1, 0)])]
    slice x6 -> x5, local copies, waits for them, and re-layouts: 4.04 us -> 1.47 us  [the longest x1 0.76 us: by_one(): g_ext[7:9]]
    pad x4 -> x0, local copies, waits for them, and re-layouts: 2.5 us -> none  [the longest x1 0.67 us: local(): ext = jnp.pad(ext, ((0, 0), (0, EXT - ext.shape[1]), (0, 0)))]
  transfers between devices with their start and end apart: 3 -> 0, of which waited for: 3 -> 0; matrix products, arithmetic and copies ran while one was open for 4% -> 0% of each run, Pallas kernels for 0% -> 0%
where the time goes in v2:
time: 183 us; the launch traced here: 182 us
  Pallas kernels  162 us (89%)
  local copies, waits for them, and re-layouts  11.1 us (6%)
  other arithmetic  8.68 us (5%)
    pallas_call x1, Pallas kernels, mega(): pl.pallas_call(functools.partial(mega_kernel, chips), out_shape=[jax.Shap...  162 us
    unnamed x54, local copies, waits for them, and re-layouts  8.94 us
    sub x6, other arithmetic, adamw(): weight - step_rate * (scaled_first / (jnp.sqrt(scaled_second) + 1e-08) +...  7.31 us

profile of v2, /device:TPU:0, one launch (start us, length us, event | category | flops | bytes accessed | tf_op | source)
XLA Modules:
  0.0 182.5 jit_solution(13815454369189647352)
XLA Ops:
  0.7 0.7 copy-done.17
  1.4 0.1 tile.9
  1.4 0.7 slice-done
  2.1 0.1 tile.21
  2.2 0.6 copy-done.18
  2.8 0.1 copy.82
  2.9 0.1 reshape.96
  3.0 0.6 select_maximum_fusion.refs_7_
  3.6 2.4 %copy.84.refs_6_ = f32[2048,64]{1,0:T(8,128)} copy(f32[2048,64]{0,1:T(8,128)} %param.27) | data formatting | bytes 1048576 | tf_op args[6]
  6.0 0.8 copy.83.refs_4_
  6.9 0.7 copy-done.24
  7.5 0.1 eq.40
  7.6 0.7 fusion.9.refs_2_
  8.4 161.8 %train_step.1 = (bf16[128,1024]{1,0:T(8,128)(2,1)}, bf16[128,1024]{1,0:T(8,128)(2,1)}, f32[64,1536]{1,0:T(8,128)}, f32[64,512]{1,0:T(8,128)}, f32[64,2048]{1,0:T...) custom-call(bf16[128,1024]{1,0:T(8,128)(2,1)} %bitcast.45, bf16[128,1024]{1,0:T(8,128)(2,1)} %bitcast.46, ...), custom_call_target="tpu_custom_call" | custom-call | tf_op jit(solution)/shard_map/train_step/pallas_call | solution.py:870
  170.2 0.8 slice.18
  171.0 0.1 constant_dynamic-slice_fusion
  171.0 0.0 copy-done.23
  171.1 0.1 reshape_squeeze.3
  171.2 0.0 copy-start.19
  171.2 0.0 copy-start.20
  171.2 0.1 copy.86
  171.3 0.6 copy-done.19
  171.9 0.0 copy-done.20
  171.9 0.6 multiply_subtract_fusion.4
  172.5 0.7 copy-done.22
  173.2 0.0 copy-done.21
  173.2 0.7 multiply_subtract_fusion.5
  173.9 0.0 copy-start
  173.9 0.0 copy-start.5
  173.9 0.0 copy-start.6
  174.0 2.6 %multiply_subtract_fusion.1 = (f32[64,2048]{1,0:T(8,128)}, f32[64,2048]{1,0:T(8,128)}, f32[64,2048]{1,0:T(8,128)}) fusion(f32[64,2048]{1,0:T(8,128)S(1)} %copy-done.1, f32[64,2048]{1,0:T(8,128)} %get-tuple-element.31, f32[64,2048]{1,0:T(8,128)S(1)} %copy-done.3, f32[64,2048]{1,0:T(8,128)S(1)} %copy-done.4), kind=kLoop, calls=%fused_computation.8 | loop fusion | flops 1966080 | bytes 3670016 | tf_op jit(solution)/shard_map/sub | solution.py:47
  176.5 0.0 copy-done
  176.5 0.0 copy-done.6
  176.5 0.0 copy-start.2
  176.6 0.0 copy-start.9
  176.6 0.0 copy-start.10
  176.6 0.0 copy-start.11
  176.6 1.4 multiply_subtract_fusion
  178.0 0.0 copy-done.9
  178.0 0.1 copy-done.10
  178.1 0.4 copy-done.11
  178.5 1.2 multiply_subtract_fusion.2
  179.7 0.0 copy-done.14
  179.7 0.8 multiply_subtract_fusion.3
  180.5 0.2 copy-done.13
  180.7 0.7 copy.94
  181.4 0.3 copy-done.12
  181.8 0.7 copy.95
  (35 shorter events, 0.1 us)
Async XLA Ops:
  0.7 0.7 copy-start.17
  1.4 0.7 slice-start
  2.1 0.7 copy-start.18
  3.6 2.4 %copy-start.8 = (f32[512,64]{0,1:T(8,128)S(1)}, f32[512,64]{0,1:T(8,128)}, u32[]{:S(2)}) copy-start(f32[512,64]{0,1:T(8,128)} %param.25) | copy-start | bytes 393220
  6.9 0.7 copy-start.24
  8.4 165.5 %copy-start.1 = (f32[64,2048]{1,0:T(8,128)S(1)}, f32[64,2048]{1,0:T(8,128)}, u32[]{:S(2)}) copy-start(f32[64,2048]{1,0:T(8,128)} %refs_5_.1) | copy-start | bytes 1572868
  8.4 165.5 %copy-start.3 = (f32[64,2048]{1,0:T(8,128)S(1)}, f32[64,2048]{1,0:T(8,128)}, u32[]{:S(2)}) copy-start(f32[64,2048]{1,0:T(8,128)} %param.32) | copy-start | bytes 1572868
  8.4 165.5 %copy-start.4 = (f32[64,2048]{1,0:T(8,128)S(1)}, f32[64,2048]{1,0:T(8,128)}, u32[]{:S(2)}) copy-start(f32[64,2048]{1,0:T(8,128)} %param.38) | copy-start | bytes 1572868
  170.2 0.9 copy-start.23
  171.2 0.7 copy-start.19
  171.2 0.7 copy-start.20
  172.5 0.7 copy-start.22
  172.5 0.7 copy-start.21
  173.9 2.6 %copy-start = (f32[2048,64]{0,1:T(8,128)S(1)}, f32[2048,64]{0,1:T(8,128)}, u32[]{:S(2)}) copy-start(f32[2048,64]{0,1:T(8,128)} %param.27) | copy-start | bytes 1572868
  173.9 2.6 %copy-start.5 = (f32[2048,64]{0,1:T(8,128)S(1)}, f32[2048,64]{0,1:T(8,128)}, u32[]{:S(2)}) copy-start(f32[2048,64]{0,1:T(8,128)} %param.33) | copy-start | bytes 1572868
  173.9 2.6 %copy-start.6 = (f32[2048,64]{0,1:T(8,128)S(1)}, f32[2048,64]{0,1:T(8,128)}, u32[]{:S(2)}) copy-start(f32[2048,64]{0,1:T(8,128)} %param.39) | copy-start | bytes 1572868
  173.9 2.6 %copy-start.7 = (f32[64,2048]{1,0:T(8,128)S(1)}, f32[64,2048]{1,0:T(8,128)}, u32[]{:S(2)}) copy-start(f32[64,2048]{1,0:T(8,128)} %get-tuple-element.32) | copy-start | bytes 1572868
  176.5 1.5 copy-start.2
  176.6 1.4 copy-start.9
  176.6 1.5 copy-start.10
  176.6 1.9 %copy-start.11 = (f32[64,1536]{1,0:T(8,128)S(1)}, f32[64,1536]{1,0:T(8,128)}, u32[]{:S(2)}) copy-start(f32[64,1536]{1,0:T(8,128)} %get-tuple-element.29) | copy-start | bytes 1179652
  178.5 1.2 copy-start.14
  178.5 1.2 copy-start.15
  178.5 1.2 copy-start.16
  179.7 1.0 copy-start.13
  180.7 1.0 copy-start.12

commit v3 on v2

--- a/solution.py
+++ b/solution.py
@@ -485,13 +485,13 @@
     terms = refs[25:30]
     left, right = refs[30:34], refs[34:38]
     (norm, split, bias, qkv, r, a2, slope, dr, ext, ext_other) = refs[38:48]
-    mine, other = refs[48:51], refs[51:54]
-    (g_send, g_recv, gs_send, gs_recv, r_send, r_recv, s_send, s_recv, m_send, m_recv) = refs[54:]
+    mine, other = refs[48:52], refs[52:56]
+    (g_send, g_recv, gs_send, gs_recv, r_send, r_recv, s_send, s_recv, m_send, m_recv) = refs[56:]
 
     count = 2 * chips
     rows = i_fc.shape[0]
     total = tokens.shape[0]
-    width = i_out.shape[0]
+    width = i_out.shape[1]
     hidden = i_fc.shape[1]
     me, sibling, place, device = ring_place(chips)
     peer = 1 - lax.axis_index("mp")
@@ -615,10 +615,10 @@
     full[4][rows_of(4, me), :] = i_ext[...].astype(BF)
     for t in range(3):
         full[0][own, pl.ds(t * width, width)] = i_qkv[t].astype(BF)
-    full[1][own, :] = i_out[...].T.astype(BF)
+    full[1][own, :] = i_out[...].astype(BF)
     gather_step(0, 0)
     full[2][own, :] = i_fc[...].astype(BF)
-    full[3][own, :] = i_proj[...].T.astype(BF)
+    full[3][own, :] = i_proj[...].astype(BF)
     left[3][:, pl.ds(0, total)] = flip(cot[...])
     here = pl.ds(0, total)
 
@@ -696,23 +696,23 @@
             copy.wait()
 
     pairs = width // (2 * HD)
-    lag = chips // 2
+    lag = 3
     units = [
         [lambda: gather_end(0), first_norm, lambda: project(0)],
-        [lambda: project(1), lambda: project(2)],
-        [lambda j=j: attend(j) for j in range(pairs)],
-        [attend_out],
+        [lambda: project(1), lambda: project(2)]
+        + [lambda j=j: attend(j) for j in range(pairs // 2)],
+        [lambda j=j: attend(j) for j in range(pairs // 2, pairs)] + [attend_out],
         [lambda: gather_end(1)],
-        [second_norm],
-        [lambda: gelu(0), lambda: gelu(1)],
-        [lambda: gelu(2), lambda: gelu(3), lambda: start_all(to_side(3))],
+        [second_norm, lambda: gelu(0)],
+        [lambda: gelu(1), lambda: gelu(2)],
+        [lambda: gelu(3), lambda: start_all(to_side(3))],
     ]
-    for tick in range(2 * lag + chips):
+    for tick in range(chips + max(2 * lag, len(units))):
         for group in range(3):
             step = tick - lag * group
             if 0 <= step < chips and (group, step) != (0, 0):
                 gather_step(group, step)
-        if tick >= chips:
+        if 0 <= tick - chips < len(units):
             for unit in units[tick - chips]:
                 unit()
     gather_end(2)
@@ -723,21 +723,22 @@
             slope[:, columns] * dot(cot[...], full[3][:, columns])
         ).astype(BF)
 
+    def feed_back():
+        mine[1][...] = dot(right[2][here, :], full[2][...], NT).astype(BF)
+        to_peer(1).start()
+
     def feed_out():
-        mine[1][:, pl.ds(0, D)] = dot(right[3][here, :], full[3][...], NT).astype(BF)
-
-    def feed_back():
-        mine[1][:, pl.ds(D, D)] = dot(right[2][here, :], full[2][...], NT).astype(BF)
-        to_peer(1).start()
+        mine[3][...] = dot(right[3][here, :], full[3][...], NT).astype(BF)
+        to_peer(3).start()
+
+    def finish_out():
+        to_peer(3).wait()
+        both = mine[3][...].astype(F32) + other[3][...].astype(F32)
+        out[...] = (r[...] + both + norm[6:7]).astype(BF)
 
     def second_back():
         to_peer(1).wait()
-        out[...] = (
-            r[...]
-            + (mine[1][:, pl.ds(0, D)].astype(F32) + other[1][:, pl.ds(0, D)].astype(F32))
-            + norm[6:7]
-        ).astype(BF)
-        da2 = mine[1][:, pl.ds(D, D)].astype(F32) + other[1][:, pl.ds(D, D)].astype(F32)
+        da2 = mine[1][...].astype(F32) + other[1][...].astype(F32)
         unit, scale = normalize(r[...])
         top = cot[...].astype(F32)
         value = top + normalize_back(da2, norm[3:4], unit, scale)
@@ -751,12 +752,12 @@
                 ext[pl.ds(d * EXT + 3 + j, 1), :] = line[:, d * rows // 128 * 128 :][:, :128]
 
     def heads_back():
-        r[:, pl.ds(0, width)] = dot(a2[...], full[1][...])
+        mine[2][:, pl.ds(0, width)] = dot(a2[...], full[1][...]).astype(BF)
 
     def attend_back(pair):
         query, key, value = heads_of(pair)
         first = pair * 2 * HD
-        do = r[:, pl.ds(first, 2 * HD)].astype(BF)
+        do = mine[2][:, pl.ds(first, 2 * HD)]
         allowed = allow[...] > 0.5
         zero = jnp.zeros_like(query)
         dq = jnp.zeros(query.shape, F32)
@@ -800,25 +801,23 @@
     ext[...] = jnp.zeros(ext.shape, F32)
     waves = (
         (members[2], 0, lambda: wait_all(to_side(3))),
-        (members[1], 3, lambda: wait_all(to_side(2))),
-        (members[0][1:], 8, lambda: wait_all(to_side(0) + to_side(1))),
-        (members[0][:1], 9, side_ext.wait),
+        (members[1], 2, lambda: wait_all(to_side(2))),
+        (members[0][3:], 5, lambda: wait_all(to_side(1))),
+        (members[0][1:3], 7, lambda: wait_all(to_side(0))),
+        (members[0][:1], 8, side_ext.wait),
     )
     units = [
-        [lambda: gate_back(0), lambda: gate_back(1), lambda: gate_back(2)]
-        + [lambda: gate_back(3), lambda: start_all(to_side(2))],
-        [feed_back, feed_out],
-        [],
-        [],
+        [lambda j=j: gate_back(j) for j in range(4)] + [lambda: start_all(to_side(2))],
+        [feed_back],
+        [feed_out],
         [second_back, lambda: start_all(to_side(1))],
         [heads_back] + [lambda j=j: attend_back(j) for j in range(pairs // 2)],
         [lambda j=j: attend_back(j) for j in range(pairs // 2, pairs)]
-        + [lambda: start_all(to_side(0))],
-        [attend_in],
+        + [lambda: start_all(to_side(0)), attend_in],
+        [finish_out],
         [first_back],
     ]
-    units[1] = [feed_out, feed_back]
-    for tick in range(9 + chips):
+    for tick in range(8 + chips):
         for ks, begin, ready in waves:
             step = tick - begin
             if step == 0:
@@ -841,7 +840,7 @@
     chips = count // 2
     total = tokens.shape[0]
     rows, hidden = w_fc.shape
-    width = w_out.shape[0]
+    width = w_out.shape[1]
     widths = (3 * width, width, hidden, hidden, 128)
     heights = (rows, rows, rows, rows, EXT)
     scratch = [pltpu.VMEM((count * h, w), BF) for h, w in zip(heights, widths)]
@@ -861,11 +860,11 @@
         pltpu.VMEM((count * EXT, 128), F32),
         pltpu.VMEM((count * EXT, 128), F32),
     ]
-    scratch += [pltpu.VMEM((total, w), BF) for w in (D, 2 * D, D)] * 2
+    scratch += [pltpu.VMEM((total, w), BF) for w in (D, D, D, D)] * 2
     n_parts = 13
     sem = pltpu.SemaphoreType.DMA
     scratch += [sem((n_parts, chips - 1))] * 2 + [sem((n_parts, chips))] * 2
-    scratch += [sem((n_parts, chips - 1))] * 2 + [sem((9,))] * 2 + [sem((3,))] * 2
+    scratch += [sem((n_parts, chips - 1))] * 2 + [sem((9,))] * 2 + [sem((4,))] * 2
     shapes = [((total, D), BF)] * 2 + [((h, w), F32) for h, w in zip(heights, widths)]
     return pl.pallas_call(
         functools.partial(mega_kernel, chips),
@@ -997,7 +996,7 @@
     piece = vec_split.shape[1]
     ext = pack_lanes(vec_norm, vec_split)
     out, in_grad, g_qkv, g_out, g_fc, g_proj, g_ext = mega(
-        count, t, cot, allow, w_qkv, w_out, w_fc, w_proj, ext
+        count, t, cot, allow, w_qkv, w_out.T, w_fc, w_proj.T, ext
     )
     reduced = (
         g_qkv.reshape(rows, 3, width).transpose(1, 0, 2),

time: 183 us -> 176 us (0.962)
  Pallas kernels: 162 us -> 158 us
  local copies, waits for them, and re-layouts: 11.1 us -> 7.92 us
    pallas_call x1, Pallas kernels: 162 us -> 158 us  [mega(): pl.pallas_call(functools.partial(mega_kernel, chips), out_shape=[jax.Shap...]
    unnamed x54 -> x52, local copies, waits for them, and re-layouts: 8.94 us -> 5.76 us
where the time goes in v3:
time: 176 us; the launch traced here: 175 us
  Pallas kernels  158 us (90%)
  other arithmetic  8.68 us (5%)
  local copies, waits for them, and re-layouts  7.92 us (4%)
    pallas_call x1, Pallas kernels, mega(): pl.pallas_call(functools.partial(mega_kernel, chips), out_shape=[jax.Shap...  158 us
    sub x6, other arithmetic, adamw(): weight - step_rate * (scaled_first / (jnp.sqrt(scaled_second) + 1e-08) +...  7.31 us
    unnamed x52, local copies, waits for them, and re-layouts  5.76 us

profile of v3, /device:TPU:0, one launch (start us, length us, event | category | flops | bytes accessed | tf_op | source)
XLA Modules:
  0.0 175.2 jit_solution(17027101436918226288)
XLA Ops:
  0.7 0.0 copy-start.17
  0.7 0.7 copy-done.17
  1.4 0.1 tile.9
  1.4 0.7 slice-done
  2.1 0.1 tile.21
  2.2 0.6 copy-done.18
  2.8 0.1 copy.76
  2.9 0.1 reshape.96
  3.0 0.6 select_maximum_fusion.refs_7_
  3.6 0.7 copy-done.24
  4.3 0.1 eq.40
  4.4 0.7 fusion.9.refs_2_
  5.1 157.7 %train_step.1 = (bf16[128,1024]{1,0:T(8,128)(2,1)}, bf16[128,1024]{1,0:T(8,128)(2,1)}, f32[64,1536]{1,0:T(8,128)}, f32[64,512]{1,0:T(8,128)}, f32[64,2048]{1,0:T...) custom-call(bf16[128,1024]{1,0:T(8,128)(2,1)} %bitcast.47, bf16[128,1024]{1,0:T(8,128)(2,1)} %bitcast.48, ...), custom_call_target="tpu_custom_call" | custom-call | tf_op jit(solution)/shard_map/train_step/pallas_call | solution.py:869
  162.9 0.0 copy-start.23
  162.9 0.8 slice.18
  163.6 0.1 constant_dynamic-slice_fusion
  163.7 0.0 copy-done.23
  163.7 0.1 reshape_squeeze.3
  163.8 0.0 copy-start.19
  163.8 0.0 copy-start.20
  163.9 0.1 copy.78
  163.9 0.6 copy-done.19
  164.5 0.0 copy-done.20
  164.5 0.6 multiply_subtract_fusion.4
  165.2 0.7 copy-done.22
  165.9 0.0 copy-done.21
  165.9 0.7 multiply_subtract_fusion.5
  166.6 0.0 copy-done
  166.6 0.0 copy-done.3
  166.6 0.0 copy-start.1
  166.6 0.0 copy-start.5
  166.6 0.0 copy-start.6
  166.6 2.6 %multiply_subtract_fusion.1 = (f32[64,2048]{1,0:T(8,128)}, f32[64,2048]{1,0:T(8,128)}, f32[64,2048]{1,0:T(8,128)}) fusion(f32[64,2048]{1,0:T(8,128)S(1)} %copy-done, f32[64,2048]{1,0:T(8,128)} %get-tuple-element.31, f32[64,2048]{1,0:T(8,128)S(1)} %copy-done.3, f32[64,2048]{1,0:T(8,128)S(1)} %copy-done.4), kind=kLoop, calls=%fused_computation.8 | loop fusion | flops 1966080 | bytes 3670016 | tf_op jit(solution)/shard_map/sub | solution.py:47
  169.2 0.0 copy-done.1
  169.2 0.0 copy-start.2
  169.2 0.0 copy-start.9
  169.2 0.0 copy-start.10
  169.3 1.4 multiply_subtract_fusion
  170.7 0.1 copy-done.10
  170.7 0.4 copy-done.11
  171.1 1.2 multiply_subtract_fusion.2
  172.4 0.0 copy-done.14
  172.4 0.0 copy-done.16
  172.4 0.8 multiply_subtract_fusion.3
  173.2 0.2 copy-done.13
  173.4 0.7 copy.86
  174.1 0.3 copy-done.12
  174.5 0.7 copy.87
  (33 shorter events, 0.1 us)
Async XLA Ops:
  0.7 0.7 copy-start.17
  1.4 0.7 slice-start
  2.1 0.7 copy-start.18
  3.6 0.7 copy-start.24
  5.1 161.4 %copy-start = (f32[64,2048]{1,0:T(8,128)S(1)}, f32[64,2048]{1,0:T(8,128)}, u32[]{:S(2)}) copy-start(f32[64,2048]{1,0:T(8,128)} %refs_5_.1) | copy-start | bytes 1572868
  5.1 161.4 %copy-start.3 = (f32[64,2048]{1,0:T(8,128)S(1)}, f32[64,2048]{1,0:T(8,128)}, u32[]{:S(2)}) copy-start(f32[64,2048]{1,0:T(8,128)} %param.32) | copy-start | bytes 1572868
  5.1 161.4 %copy-start.4 = (f32[64,2048]{1,0:T(8,128)S(1)}, f32[64,2048]{1,0:T(8,128)}, u32[]{:S(2)}) copy-start(f32[64,2048]{1,0:T(8,128)} %param.38) | copy-start | bytes 1572868
  162.9 0.9 copy-start.23
  163.8 0.7 copy-start.19
  163.8 0.7 copy-start.20
  165.2 0.7 copy-start.22
  165.2 0.7 copy-start.21
  166.6 2.6 %copy-start.1 = (f32[2048,64]{0,1:T(8,128)S(1)}, f32[2048,64]{0,1:T(8,128)}, u32[]{:S(2)}) copy-start(f32[2048,64]{0,1:T(8,128)} %param.27) | copy-start | bytes 1572868
  166.6 2.6 %copy-start.5 = (f32[2048,64]{0,1:T(8,128)S(1)}, f32[2048,64]{0,1:T(8,128)}, u32[]{:S(2)}) copy-start(f32[2048,64]{0,1:T(8,128)} %param.33) | copy-start | bytes 1572868
  166.6 2.6 %copy-start.6 = (f32[2048,64]{0,1:T(8,128)S(1)}, f32[2048,64]{0,1:T(8,128)}, u32[]{:S(2)}) copy-start(f32[2048,64]{0,1:T(8,128)} %param.39) | copy-start | bytes 1572868
  166.6 2.6 %copy-start.7 = (f32[64,2048]{1,0:T(8,128)S(1)}, f32[64,2048]{1,0:T(8,128)}, u32[]{:S(2)}) copy-start(f32[64,2048]{1,0:T(8,128)} %get-tuple-element.32) | copy-start | bytes 1572868
  169.2 1.5 copy-start.2
  169.2 1.4 copy-start.9
  169.2 1.5 copy-start.10
  169.2 1.9 %copy-start.11 = (f32[64,1536]{1,0:T(8,128)S(1)}, f32[64,1536]{1,0:T(8,128)}, u32[]{:S(2)}) copy-start(f32[64,1536]{1,0:T(8,128)} %get-tuple-element.29) | copy-start | bytes 1179652
  171.1 1.2 copy-start.8
  171.1 1.2 copy-start.14
  171.1 1.2 copy-start.15
  171.1 1.3 copy-start.16
  172.4 1.0 copy-start.13
  173.4 1.0 copy-start.12
